TPU v7x, 256 devices: a whole 4x4x8 slice. The times are simulated.
256 devices in a mesh: role: 2 (over core), grp: 8 (over z_hi, y), tp: 16 (over z_lo, x).
Axes of the slice: x: 4, y: 4, z: 8 (z_hi: 2, z_lo: 4; z = z_hi * 4 + z_lo), core: 2. Of those that a mesh axis runs over, the one named last changes fastest.
Arguments:
- residual: bfloat16 [2, 1024, 3584], P('role', 'grp', 'tp'), may hold values from -300 to 300
- queries: bfloat16 [2, 1024, 4096], P('role', 'grp', 'tp'), may hold values from -200 to 200
- kv_cache: bfloat16 [2, 1024, 16, 256], P('role', 'grp'), may hold values from -8 to 8
- cache_lengths: int32 [2, 1024], P('role', 'grp'), may hold values from 2 to 16, as said below
- out_proj: bfloat16 [4096, 3584], P('tp'), may hold values from -0.125 to 0.125
- norm_gain: bfloat16 [3584], replicated, may hold values from 0.099609375 to 1.8984375
- routes: int32 [2, 1024, 3], P('role', 'grp'), may hold values from 0 to 31, all different within a row; in each aligned block of 128 rows (0 to 127, 128 to 255, ..., all dimensions but the last counted through in order) at most 24 rows name the same one
- gate_weights: float32 [2, 1024, 3], P('role', 'grp'), may hold values from 0.2 to 1
- expert_in: bfloat16 [32, 2, 2560, 3584], P(('role', 'grp'), None, 'tp'), may hold values from -0.09375 to 0.09375
- expert_out: bfloat16 [32, 2560, 3584], P(('role', 'grp'), 'tp'), may hold values from -0.15625 to 0.15625
- shared_in: bfloat16 [2, 2560, 3584], P(None, 'tp'), may hold values from -0.09375 to 0.09375
- shared_out: bfloat16 [2560, 3584], P('tp'), may hold values from -0.15625 to 0.15625
Outputs:
- layer_out: bfloat16 [2, 1024, 3584], P('role', 'grp', 'tp')
Inputs may be any that keep to these rules, and one draw needn't show every extreme that they name: `routes`: each row names 3 different experts. In every aligned block of 128 rows of one micro-batch (the rows of one data group) no expert is named by more than 24 rows, and in some block one expert is named by exactly 24 rows. `cache_lengths`: in every aligned block of 128 rows of one micro-batch some row has length 16.
All inputs are finite; a program needn't handle non-finite values.
Results may differ from a plain program's by a relative error of at most 0.0058.
Values may be sent and summed in bfloat16 or wider, within the bound.
A program may use at most 128 MiB of HBM per device.

v0:
```python
import jax
import jax.numpy as jnp
from jax import lax
from jax.sharding import PartitionSpec as P

HD = 128
EXPERTS = 32
TOPK = 3
L = 16
CAP = 24


def slot_places(routes_local, capacity, expert_count):
    row_count, choose_count = routes_local.shape
    flat_routes = routes_local.reshape(row_count * choose_count)
    expert_ids = jnp.arange(expert_count, dtype=jnp.int32)
    onehot = (flat_routes[:, None] == expert_ids[None, :]).astype(jnp.int32)
    before = jnp.cumsum(onehot, axis=0) - onehot
    position = jnp.sum(before * onehot, axis=1)
    slot_index = flat_routes * capacity + position
    return slot_index.reshape(row_count, choose_count)


def combine_slots(slot_table, slot_index, flat_gates):
    routed = flat_gates[:, 0:1] * slot_table[slot_index[:, 0]].astype(jnp.float32)
    for choose in range(1, TOPK):
        routed = routed + flat_gates[:, choose : choose + 1] * slot_table[
            slot_index[:, choose]
        ].astype(jnp.float32)
    return routed


def body(
    residual,
    queries,
    kv_cache,
    cache_lengths,
    out_proj,
    norm_gain,
    routes,
    gate_weights,
    expert_in,
    expert_out,
    shared_in,
    shared_out,
):
    row_count = residual.shape[1]
    width_part = residual.shape[2]
    model_width = width_part * lax.axis_size("tp")
    head_count = queries.shape[2] // HD
    query_heads = queries.reshape(row_count, head_count, HD)
    cache_rows = kv_cache.reshape(row_count, L, 2 * HD)
    cache_keys = cache_rows[:, :, :HD]
    cache_values = cache_rows[:, :, HD:]
    scores = jnp.einsum(
        "rhd,rld->rhl", query_heads, cache_keys, preferred_element_type=jnp.float32
    ) * HD ** (-0.5)
    visible = (
        jnp.arange(L, dtype=jnp.int32)[None, None, :]
        < cache_lengths.reshape(row_count)[:, None, None]
    )
    scores = jnp.where(visible, scores, -1e30)
    maximum = jnp.max(scores, axis=-1, keepdims=True)
    exponent = jnp.where(visible, jnp.exp(scores - maximum), 0.0)
    attn_weights = (exponent / jnp.sum(exponent, axis=-1, keepdims=True)).astype(jnp.bfloat16)
    context = jnp.einsum(
        "rhl,rld->rhd", attn_weights, cache_values, preferred_element_type=jnp.float32
    ).astype(jnp.bfloat16)
    attended = jnp.dot(
        context.reshape(row_count, head_count * HD), out_proj, preferred_element_type=jnp.float32
    )
    residual_part = residual.reshape(row_count, width_part)
    summed = lax.psum_scatter(attended, "tp", scatter_dimension=1, tiled=True)
    hidden_part = (residual_part.astype(jnp.float32) + summed).astype(jnp.bfloat16)
    hidden = lax.all_gather(hidden_part, "tp", axis=1, tiled=True)
    hidden_wide = hidden.astype(jnp.float32)
    mean_square = jnp.mean(hidden_wide * hidden_wide, axis=-1, keepdims=True)
    normed = (hidden_wide * lax.rsqrt(mean_square + 1e-06) * norm_gain.astype(jnp.float32)).astype(
        jnp.bfloat16
    )
    shared_pre = jnp.einsum("rd,gfd->rgf", normed, shared_in, preferred_element_type=jnp.float32)
    shared_act = (jax.nn.silu(shared_pre[:, 0]) * shared_pre[:, 1]).astype(jnp.bfloat16)
    shared_partial = jnp.dot(shared_act, shared_out, preferred_element_type=jnp.float32)
    owner_count = lax.axis_size(("role", "grp"))
    local_experts = expert_in.shape[0]
    slot_index = slot_places(routes.reshape(row_count, TOPK), CAP, EXPERTS)
    slot_ids = jnp.arange(EXPERTS * CAP, dtype=jnp.int32)
    dispatch = jnp.any(slot_ids[:, None, None] == slot_index[None, :, :], axis=2).astype(
        jnp.bfloat16
    )
    outgoing = jnp.dot(dispatch, normed, preferred_element_type=jnp.float32).astype(jnp.bfloat16)
    outgoing = outgoing.reshape(owner_count, local_experts, CAP, model_width)
    arrived = lax.all_to_all(outgoing, ("role", "grp"), split_axis=0, concat_axis=0, tiled=True)
    expert_pre = jnp.einsum(
        "sjcd,jgfd->sjcgf", arrived, expert_in, preferred_element_type=jnp.float32
    )
    expert_act = (jax.nn.silu(expert_pre[..., 0, :]) * expert_pre[..., 1, :]).astype(jnp.bfloat16)
    produced = jnp.einsum(
        "sjcf,jfd->sjcd", expert_act, expert_out, preferred_element_type=jnp.float32
    ).astype(jnp.bfloat16)
    flat_gates = gate_weights.reshape(row_count, TOPK)
    returned = lax.all_to_all(produced, ("role", "grp"), split_axis=0, concat_axis=0, tiled=True)
    slot_table = returned.reshape(EXPERTS * CAP, model_width)
    routed = combine_slots(slot_table, slot_index, flat_gates)
    branches = lax.psum_scatter(shared_partial + routed, "tp", scatter_dimension=1, tiled=True)
    layer_out = (hidden_part.astype(jnp.float32) + branches).astype(jnp.bfloat16)
    return layer_out.reshape(1, row_count, width_part)


def solution(mesh):
    in_specs = (
        P("role", "grp", "tp"),
        P("role", "grp", "tp"),
        P("role", "grp", None, None),
        P("role", "grp"),
        P("tp", None),
        P(),
        P("role", "grp", None),
        P("role", "grp", None),
        P(("role", "grp"), None, "tp", None),
        P(("role", "grp"), "tp", None),
        P(None, "tp", None),
        P("tp", None),
    )
    out_specs = P("role", "grp", "tp")
    return jax.shard_map(body, mesh=mesh, in_specs=in_specs, out_specs=out_specs, check_vma=False)
```

profile of v0, /device:TPU:1, one launch (start us, length us, event | category | flops | bytes accessed | tf_op | source)
XLA Modules:
  0.0 525.2 jit_solution(1392625341501602589)
XLA Ops:
  6.5 0.0 copy-start
  6.5 0.0 copy-start.6
  6.5 0.0 reduce-scatter.3.cloned.1.call-start
  6.5 0.9 iota_compare_fusion.1
  7.4 0.9 reshape.82
  8.4 2.2 fusion.48
  10.6 0.0 copy-start.1
  10.6 0.0 copy-done.6
  10.6 1.3 convolution_convert_fusion.2
  11.9 0.2 copy-done.1
  12.1 2.1 fusion.35
  14.2 0.0 copy-start.5
  14.2 0.0 copy-start.3
  14.2 0.0 copy-start.2
  14.2 0.0 reduce-scatter.3.cloned.1.call-update
  14.3 0.7 copy-done.5
  14.9 0.1 copy.54
  15.0 0.2 eq.45
  15.2 0.2 eq.41
  15.4 0.0 copy-done.3
  15.5 0.9 reduce-window.6
  16.4 0.2 slice_reduce_fusion
  16.6 0.1 fusion.42
  16.7 0.2 reduce_sum.34
  17.0 0.1 copy.58
  17.0 0.2 fusion.14
  17.2 78.0 %reduce-scatter.3.cloned.1.call-done = f32[128,224]{0,1:T(8,128)} async-done(((f32[128,3584]{0,1:T(8,128)}), f32[128,224]{0,1:T(8,128)}) %reduce-scatter.3.cloned.1.call-update) | async-done | bytes 114704 | tf_op jit(solution)/shard_map/reduce_scatter | solution.py:73
  95.2 0.0 copy-done.2
  95.2 0.9 fusion.29
  96.1 36.0 %all_gather.3 = bf16[128,3584]{0,1:T(8,128)(2,1)S(1)} all-gather(bf16[128,224]{0,1:T(8,128)(2,1)S(1)} %fusion.29), channel_id=1, replica_groups=mesh['role'=2,'grp'=8,'tp'=16] {'tp'}, dimensions={1}, use_global_device_ids=true | all-gather | bytes 974848 | tf_op jit(solution)/shard_map/all_gather | solution.py:75
  132.2 0.5 fusion.6
  132.7 0.0 slice-start
  132.7 2.5 convolution_convert_fusion
  135.2 0.0 slice-start.1
  135.2 139.1 %all_to_all.10 = bf16[16,2,24,3584]{3,2,1,0:T(8,128)(2,1)S(1)} all-to-all(bf16[16,2,24,3584]{3,2,1,0:T(8,128)(2,1)S(1)} %bitcast.100), channel_id=1, replica_groups=mesh['role'=2,'grp'=8,'tp'=16] {'role','grp'}, dimensions={0} | all-to-all | bytes 11010048 | tf_op jit(solution)/shard_map/all_to_all | solution.py:93
  274.4 0.0 slice-done
  274.4 0.0 slice-done.1
  274.4 3.2 fusion.9
  277.6 0.0 copy-done
  277.6 1.6 fusion.1
  279.2 3.0 copy.61
  282.3 0.0 copy-start.4
  282.3 7.4 %all-to-all-start.1 = ((bf16[16,2,24,3584]{3,2,1,0:T(8,128)(2,1)}), bf16[16,2,24,3584]{3,2,1,0:T(8,128)(2,1)}, u32[]{:S(2)}, u32[]{:S(2)}) async-start(bf16[16,2,24,3584]{3,2,1,0:T(8,128)(2,1)} %copy.61), calls=%async_computation.2 | async-start | bytes 11010048 | tf_op jit(solution)/shard_map/all_to_all | solution.py:102
  289.7 0.2 reduce-scatter.5.cloned.1.call-start
  289.9 0.2 reduce_sum.35
  290.1 0.0 copy-done.4
  290.2 0.2 fusion.32
  290.4 2.5 fusion.19
  292.9 119.0 %all-to-all-done.1 = bf16[16,2,24,3584]{3,2,1,0:T(8,128)(2,1)} async-done(((bf16[16,2,24,3584]{3,2,1,0:T(8,128)(2,1)}), bf16[16,2,24,3584]{3,2,1,0:T(8,128)(2,1)}, u32[]{:S(2)}, u32[]{:S(2)}) %all-to-all-start.1) | async-done | bytes 5505056 | tf_op jit(solution)/shard_map/all_to_all | solution.py:102
  412.0 5.3 %gather_fusion.2 = bf16[128,3584]{1,0:T(8,128)(2,1)S(1)} fusion(bf16[768,3584]{1,0:T(8,128)(2,1)} %bitcast.19, s32[1024]{0:T(1024)S(1)} %get-tuple-element.13), kind=kCustom, calls=%fused_computation.2 | custom fusion | bytes 1835520 | tf_op jit(solution)/shard_map/gather | solution.py:27
  417.3 1.3 copy.64
  418.5 5.3 %gather_fusion.1 = bf16[128,3584]{1,0:T(8,128)(2,1)S(1)} fusion(bf16[768,3584]{1,0:T(8,128)(2,1)} %bitcast.19, s32[1024]{0:T(1024)S(1)} %get-tuple-element.14), kind=kCustom, calls=%fused_computation.1 | custom fusion | bytes 1835520 | tf_op jit(solution)/shard_map/gather | solution.py:27
  423.8 6.3 %gather_fusion = bf16[128,3584]{1,0:T(8,128)(2,1)} fusion(bf16[768,3584]{1,0:T(8,128)(2,1)} %bitcast.19, s32[1024]{0:T(1024)S(1)} %pad_clamp_fusion.2), kind=kCustom, calls=%fused_computation | custom fusion | bytes 1835520 | tf_op jit(solution)/shard_map/gather | solution.py:25
  430.1 2.2 copy.62
  432.3 1.3 copy.63
  433.6 4.3 convolution_add_fusion
  437.9 0.0 reduce-scatter.5.cloned.1.call-update
  437.9 78.9 %reduce-scatter.5.cloned.1.call-done = f32[128,224]{0,1:T(8,128)} async-done(((f32[128,3584]{0,1:T(8,128)}), f32[128,224]{0,1:T(8,128)}) %reduce-scatter.5.cloned.1.call-update) | async-done | bytes 114704 | tf_op jit(solution)/shard_map/reduce_scatter | solution.py:105
  516.9 1.5 fusion.39
  (11 shorter events, 0.1 us)
Async XLA Ops:
  6.5 271.0 %copy-start = (bf16[2,160,3584]{2,1,0:T(8,128)(2,1)S(1)}, bf16[2,160,3584]{2,1,0:T(8,128)(2,1)}, u32[]{:S(2)}) copy-start(bf16[2,160,3584]{2,1,0:T(8,128)(2,1)} %param.21) | copy-start | bytes 6881284
  6.5 4.0 copy-start.6
  6.5 88.7 %reduce-scatter.3.cloned.1.call-start = ((), (), s32[]{:S(2)}) async-start(), calls=%async_computation.4 | async-start | bytes 1949696 | tf_op jit(solution)/shard_map/reduce_scatter | solution.py:73
  10.6 1.5 copy-start.1
  14.2 0.7 copy-start.5
  14.2 1.2 copy-start.3
  14.2 81.0 %copy-start.2 = (bf16[1,128,224]{1,2,0:T(8,128)(2,1)S(1)}, bf16[1,128,224]{1,2,0:T(8,128)(2,1)}, u32[]{:S(2)}) copy-start(bf16[1,128,224]{1,2,0:T(8,128)(2,1)} %param.12) | copy-start | bytes 172036
  132.7 141.7 %slice-start = ((s8[4587520]{0:T(1024)(128)(4,1)}), s8[4194304]{0:T(1024)(128)(4,1)S(1)}, s32[]{:S(2)}) async-start(s8[4587520]{0:T(1024)(128)(4,1)} %bitcast.105), calls=%async_computation.6 | async-start | bytes 8388608
  135.2 139.2 %slice-start.1 = ((s8[4587520]{0:T(1024)(128)(4,1)}), s8[393216]{0:T(1024)(128)(4,1)S(1)}, s32[]{:S(2)}) async-start(s8[4587520]{0:T(1024)(128)(4,1)} %bitcast.105), calls=%async_computation.7 | async-start | bytes 786432
  282.3 7.9 %copy-start.4 = (f32[1,128,3]{1,0,2:T(1,128)S(1)}, f32[1,128,3]{1,0,2:T(1,128)}, u32[]{:S(2)}) copy-start(f32[1,128,3]{1,0,2:T(1,128)} %param.19) | copy-start | bytes 4612
  282.3 129.7 %all-to-all-start.1 = ((bf16[16,2,24,3584]{3,2,1,0:T(8,128)(2,1)}), bf16[16,2,24,3584]{3,2,1,0:T(8,128)(2,1)}, u32[]{:S(2)}, u32[]{:S(2)}) async-start(bf16[16,2,24,3584]{3,2,1,0:T(8,128)(2,1)} %copy.61), calls=%async_computation.2 | async-start | bytes 11010048 | tf_op jit(solution)/shard_map/all_to_all | solution.py:102
  289.7 227.2 %reduce-scatter.5.cloned.1.call-start = ((), (), s32[]{:S(2)}) async-start(), calls=%async_computation.5 | async-start | bytes 1949696 | tf_op jit(solution)/shard_map/reduce_scatter | solution.py:105
Sparse Core Ops, SparseCore 0:
  14.4 80.7 reduce-scatter.2
  438.0 78.7 reduce-scatter.4
where the time goes:
time: 535 us; the launch traced here: 525 us
  waiting for transfers between devices  276 us (52%)
  blocking collectives  175 us (33%)
  local copies, waits for them, and re-layouts  27.7 us (5%)
  matrix products  19.9 us (4%)
  between operations  13.6 us (3%)
  starting transfers between devices  7.66 us (1%)
    all_to_all x1, blocking collectives, body(): lax.all_to_all(outgoing, ('role', 'grp'), split_axis=0, concat_axis=0, ti...  139 us
    all_to_all x1, waiting for transfers between devices, body(): lax.all_to_all(produced, ('role', 'grp'), split_axis=0, concat_axis=0, ti...  119 us
    reduce_scatter x1, waiting for transfers between devices, body(): lax.psum_scatter(shared_partial + routed, 'tp', scatter_dimension=1, tile...  78.9 us
    reduce_scatter x1, waiting for transfers between devices, body(): summed = lax.psum_scatter(attended, 'tp', scatter_dimension=1, tiled=True)  78 us
    all_gather x1, blocking collectives, body(): hidden = lax.all_gather(hidden_part, 'tp', axis=1, tiled=True)  36 us
    gather x4, local copies, waits for them, and re-layouts, combine_slots(): slot_table[slot_index[:, choose]].astype(jnp.float32)  13.1 us
  transfers between devices with their start and end apart: 3, of which 3 were waited for; matrix products, arithmetic and copies ran while one was open for 1% of the time, Pallas kernels for 0%

commit v1 on v0

v1 whole, which is shorter than its diff:
```python
import functools

import jax
import jax.numpy as jnp
from jax import lax
from jax.experimental import pallas as pl
from jax.experimental.pallas import tpu as pltpu
from jax.sharding import PartitionSpec as P

HD = 128
EXPERTS = 32
TOPK = 3
L = 16
CAP = 24
UNIT = 2 * CAP
MESH = pl.DeviceIdType.MESH
BF16 = jnp.bfloat16
F32 = jnp.float32
VMEM_LIMIT = 50 * 1024 * 1024


def places():
    role, grp, tp = lax.axis_index("role"), lax.axis_index("grp"), lax.axis_index("tp")
    return role, grp // 4, grp % 4, tp // 4, tp % 4


def flip(a, b):
    return (a + b) % 2


def xor4(a, b):
    return 2 * flip(a // 2, b // 2) + flip(a % 2, b % 2)


def z_mates(z):
    return {1: xor4(z, 1), 2: (z + 2) % 4, 3: 3 - z}


def device(role, zh, y, z, x):
    return {"role": role, "grp": zh * 4 + y, "tp": z * 4 + x}


def partners(role, zh, y, z, x):
    there = (flip(role, x % 2), 1 - zh)
    return device(*there, xor4(y, z), 3 - z, x), device(*there, xor4(y, 3 - z), 3 - z, x)


def meet(devices):
    barrier = pltpu.get_barrier_semaphore()
    for one in devices:
        pl.semaphore_signal(barrier, inc=1, device_id=one, device_id_type=MESH)
    pl.semaphore_wait(barrier, len(devices))


def plane_mates(role, zh, y, z, x):
    mates = [device(role, zh, y, z, (x + 1) % 4), device(role, zh, y, z, (x + 3) % 4)]
    return mates + [device(role, zh, y, one, x) for one in z_mates(z).values()]


def column_mates(role, zh, y, z, x):
    mates = [device(one, zh, (y + step) % 4, z, x) for step in (1, 3) for one in (0, 1)]
    return mates + [device(1 - role, zh, y, z, x)]


def send(src, dst, send_sem, recv_sem, to):
    copy = pltpu.make_async_remote_copy(
        src_ref=src, dst_ref=dst, send_sem=send_sem, recv_sem=recv_sem, device_id=to, device_id_type=MESH
    )
    copy.start()
    return copy


class PlaneSum:
    def __init__(self, here, part, half, rx1, tx, rx2, zt, zrx, s1, r1, s2, r2, zs, zr):
        self.here, self.part, self.half = here, part, half
        self.rx1, self.tx, self.rx2, self.zt, self.zrx = rx1, tx, rx2, zt, zrx
        self.s1, self.r1, self.s2, self.r2, self.zs, self.zr = s1, r1, s2, r2, zs, zr
        role, zh, y, z, x = here
        mates = z_mates(z)
        self.order = [mates[2], mates[3], mates[1], z]
        self.right, self.left = (x + 1) % 4, (x + 3) % 4
        self.to_right = device(role, zh, y, z, self.right)
        self.to_left = device(role, zh, y, z, self.left)
        self.copies = []
        self.first, self.second, self.zcopies = {}, {}, []

    def begin(self, i):
        x = self.here[4]
        far = (x + 2) % 4
        base = self.order[i] * 4
        for d, (to, near) in enumerate(((self.to_right, self.right), (self.to_left, self.left))):
            self.first[i, d] = send(
                self.half(self.part, base + far, d), self.rx1.at[i, d], self.s1.at[i, d], self.r1.at[i, d], to
            )
            self.second[i, d, 1 - d] = send(
                self.half(self.part, base + near, 1 - d),
                self.rx2.at[i, d, 1 - d],
                self.s2.at[i, d, 1 - d],
                self.r2.at[i, d, 1 - d],
                to,
            )

    def middle(self, i):
        base = self.order[i] * 4
        for d, (to, near) in enumerate(((self.to_right, self.right), (self.to_left, self.left))):
            self.first[i, d].wait_recv()
            own = self.half(self.part, base + near, d)[...]
            self.tx[i, d] = (self.rx1[i, d].astype(F32) + own.astype(F32)).astype(BF16)
            self.second[i, d, d] = send(
                self.tx.at[i, d], self.rx2.at[i, d, d], self.s2.at[i, d, d], self.r2.at[i, d, d], to
            )

    def line(self, i, h):
        x = self.here[4]
        own = self.half(self.part, self.order[i] * 4 + x, h)[...].astype(F32)
        return own + self.rx2[i, 0, h].astype(F32) + self.rx2[i, 1, h].astype(F32)

    def end(self, i):
        role, zh, y, z, x = self.here
        for d in range(2):
            for h in range(2):
                self.second[i, d, h].wait_recv()
        if i == 3:
            return
        for h in range(2):
            self.zt[i, h] = self.line(i, h).astype(BF16)
            self.zcopies.append(
                send(
                    self.zt.at[i, h],
                    self.zrx.at[i, h],
                    self.zs.at[i, h],
                    self.zr.at[i, h],
                    device(role, zh, y, self.order[i], x),
                )
            )

    def total(self, h):
        for i in range(3):
            self.zcopies[2 * i + h].wait_recv()
        value = self.line(3, h)
        for i in range(3):
            value = value + self.zrx[i, h].astype(F32)
        return value

    def drain(self):
        for copy in list(self.first.values()) + list(self.second.values()) + self.zcopies:
            copy.wait_send()

    def whole(self, between=lambda: None):
        for i in range(4):
            self.begin(i)
        self.middle(0)
        self.middle(1)
        between()
        self.end(0)
        self.middle(2)
        self.end(1)
        self.middle(3)
        self.end(2)
        self.end(3)


def plane_sum_scratch(half):
    dma = pltpu.SemaphoreType.DMA
    return [
        pltpu.VMEM((4, 2) + half, BF16),
        pltpu.VMEM((4, 2) + half, BF16),
        pltpu.VMEM((4, 2, 2) + half, BF16),
        pltpu.VMEM((3, 2) + half, BF16),
        pltpu.VMEM((3, 2) + half, BF16),
        dma((4, 2)),
        dma((4, 2)),
        dma((4, 2, 2)),
        dma((4, 2, 2)),
        dma((3, 2)),
        dma((3, 2)),
    ]


class PlaneGather:
    def __init__(self, here, out, half, zs, zr, xs, xr, fs, fr):
        self.here, self.out, self.half = here, out, half
        self.zs, self.zr, self.xs, self.xr, self.fs, self.fr = zs, zr, xs, xr, fs, fr
        role, zh, y, z, x = here
        mates = z_mates(z)
        self.order = [z, mates[1], mates[2], mates[3]]
        self.to_right = device(role, zh, y, z, (x + 1) % 4)
        self.to_left = device(role, zh, y, z, (x + 3) % 4)
        self.zcopies, self.near, self.far = {}, {}, {}

    def begin(self):
        role, zh, y, z, x = self.here
        mine = z * 4 + x
        self.start(0)
        for m in (3, 2, 1):
            for h in range(2):
                block = self.half(self.out, mine, h)
                self.zcopies[m, h] = send(
                    block, block, self.zs.at[m - 1, h], self.zr.at[m - 1, h], device(role, zh, y, self.order[m], x)
                )

    def start(self, i):
        x = self.here[4]
        slot = self.order[i] * 4 + x
        if i > 0:
            for h in range(2):
                self.zcopies[i, h].wait_recv()
        for h in range(2):
            for d, to in enumerate((self.to_right, self.to_left)):
                block = self.half(self.out, slot, h if d == 0 else 1 - h)
                k = h if d == 0 else 1 - h
                self.near[i, d, k] = send(block, block, self.xs.at[i, d, k], self.xr.at[i, d, k], to)

    def pass_on(self, i):
        x = self.here[4]
        base = self.order[i] * 4
        for d, (to, slot) in enumerate(((self.to_right, (x + 3) % 4), (self.to_left, (x + 1) % 4))):
            self.near[i, d, d].wait_recv()
            block = self.half(self.out, base + slot, d)
            self.far[i, d] = send(block, block, self.fs.at[i, d], self.fr.at[i, d], to)

    def finish(self):
        for (i, d, k), copy in self.near.items():
            if k != d:
                copy.wait_recv()
        for copy in self.far.values():
            copy.wait_recv()
        for copies in (self.zcopies, self.near, self.far):
            for copy in copies.values():
                copy.wait_send()

    def whole(self, between=lambda: None):
        self.begin()
        self.pass_on(0)
        self.start(1)
        between()
        self.start(2)
        self.pass_on(1)
        self.start(3)
        self.pass_on(2)
        self.pass_on(3)
        self.finish()


def plane_gather_scratch():
    dma = pltpu.SemaphoreType.DMA
    return [dma((3, 2)), dma((3, 2)), dma((4, 2, 2)), dma((4, 2, 2)), dma((4, 2)), dma((4, 2))]


class ColumnSwap:
    def __init__(self, here, src, dst, relay, s_near, r_near, s_rel, r_rel, s_fwd, r_fwd, s_own, r_own):
        self.here, self.src, self.dst, self.relay = here, src, dst, relay
        self.sems = (s_near, r_near, s_rel, r_rel, s_fwd, r_fwd, s_own, r_own)
        self.rel, self.fwd, self.near = {}, {}, {}

    def begin(self):
        role, zh, y, z, x = self.here
        s_near, r_near, s_rel, r_rel, s_fwd, r_fwd, s_own, r_own = self.sems
        width = self.src.shape[3] // 2
        for q in range(2):
            for d, step in enumerate((1, 3)):
                self.rel[d, q] = send(
                    self.src.at[q, (y + 2) % 4, :, pl.ds(d * width, width)],
                    self.relay.at[d, q],
                    s_rel.at[d, q],
                    r_rel.at[d, q],
                    device(role, zh, (y + step) % 4, z, x),
                )
        for q in range(2):
            for d, step in enumerate((1, 3)):
                other = (y + step) % 4
                self.near[d, q] = send(
                    self.src.at[q, other],
                    self.dst.at[role, y],
                    s_near.at[d, q],
                    r_near.at[d, role],
                    device(q, zh, other, z, x),
                )
        self.core = send(
            self.src.at[1 - role, y], self.dst.at[role, y], s_own.at[0], r_own.at[0], device(1 - role, zh, y, z, x)
        )
        self.own = pltpu.make_async_copy(self.src.at[role, y], self.dst.at[role, y], s_own.at[1])
        self.own.start()

    def pass_on(self):
        role, zh, y, z, x = self.here
        s_near, r_near, s_rel, r_rel, s_fwd, r_fwd, s_own, r_own = self.sems
        width = self.src.shape[3] // 2
        for q in range(2):
            for d, step in enumerate((1, 3)):
                self.rel[d, q].wait_recv()
                origin = (y + 4 - step) % 4
                self.fwd[d, q] = send(
                    self.relay.at[d, q],
                    self.dst.at[role, origin, :, pl.ds(d * width, width)],
                    s_fwd.at[d, q],
                    r_fwd.at[d, role],
                    device(q, zh, (y + step) % 4, z, x),
                )

    def finish(self):
        role, zh, y, z, x = self.here
        s_near, r_near, s_rel, r_rel, s_fwd, r_fwd, s_own, r_own = self.sems
        width = self.src.shape[3] // 2
        for q in range(2):
            for d, step in enumerate((1, 3)):
                block = self.dst.at[q, (y + 4 - step) % 4]
                pltpu.make_async_copy(block, block, r_near.at[d, q]).wait()
                block = self.dst.at[q, (y + 2) % 4, :, pl.ds(d * width, width)]
                pltpu.make_async_copy(block, block, r_fwd.at[d, q]).wait()
        self.core.wait_recv()
        self.own.wait()
        for copies in (self.rel, self.fwd, self.near):
            for copy in copies.values():
                copy.wait_send()
        self.core.wait_send()


def column_scratch(rows, width):
    dma = pltpu.SemaphoreType.DMA
    return [pltpu.VMEM((2, 2, rows, width // 2), BF16)] + [dma((2, 2))] * 6 + [dma((2,))] * 2


def row_half(ref, slot, h):
    rows = ref.shape[1] // 2
    return ref.at[slot, pl.ds(h * rows, rows), :]


def lane_half(ref, slot, h):
    width = ref.shape[2] // 2
    return ref.at[slot, :, pl.ds(h * width, width)]


def hidden_kernel(part, resid, out, *scratch):
    here = places()
    meet(plane_mates(*here))
    mine = here[3] * 4 + here[4]
    sums = PlaneSum(here, part, row_half, *scratch[:11])
    sums.whole()
    rows = resid.shape[0] // 2
    for h in range(2):
        value = sums.total(h) + resid[pl.ds(h * rows, rows), :].astype(F32)
        out[mine, pl.ds(h * rows, rows), :] = value.astype(BF16)
    PlaneGather(here, out, row_half, *scratch[11:]).whole()
    sums.drain()


def output_kernel(part, hidden, out, *scratch):
    here = places()
    meet(plane_mates(*here))
    sums = PlaneSum(here, part, row_half, *scratch)
    sums.whole()
    rows = hidden.shape[0] // 2
    for h in range(2):
        value = sums.total(h) + hidden[pl.ds(h * rows, rows), :].astype(F32)
        out[pl.ds(h * rows, rows), :] = value.astype(BF16)
    sums.drain()


def dispatch_kernel(same, cross, got_same, got_cross, swap_s, swap_r, *scratch):
    here = places()
    role, zh, y, z, x = here
    to, source = partners(*here)
    meet(plane_mates(*here) + column_mates(*here) + [to, source])
    swap = send(cross, got_cross.at[(3 - z) * 4 + x], swap_s.at[0], swap_r.at[0], to)
    column = ColumnSwap(here, same, got_same, *scratch[:9])
    column.begin()
    swap.wait_recv()
    gather = PlaneGather(here, got_cross, lane_half, *scratch[9:])
    gather.whole(between=column.pass_on)
    column.finish()
    swap.wait_send()


def return_kernel(same, cross, got_same, got_cross, done, swap_s, swap_r, *scratch):
    here = places()
    to, source = partners(*here)
    meet(plane_mates(*here) + column_mates(*here) + [to, source])
    column = ColumnSwap(here, same, got_same, *scratch[:9])
    sums = PlaneSum(here, cross, lane_half, *scratch[9:])
    for i in range(1):
        sums.begin(i)
    column.begin()
    for i in range(1, 4):
        sums.begin(i)
    sums.middle(0)
    sums.middle(1)
    column.pass_on()
    sums.end(0)
    sums.middle(2)
    sums.end(1)
    sums.middle(3)
    sums.end(2)
    sums.end(3)
    width = done.shape[1] // 2
    for h in range(2):
        done[:, pl.ds(h * width, width)] = sums.total(h).astype(BF16)
    swap = send(done, got_cross, swap_s.at[0], swap_r.at[0], source)
    column.finish()
    sums.drain()
    swap.wait()


def call(kernel, collective_id, out_shape, scratch, *operands):
    vmem = pl.BlockSpec(memory_space=pltpu.VMEM)
    many = isinstance(out_shape, (list, tuple))
    return pl.pallas_call(
        kernel,
        out_shape=out_shape,
        in_specs=[vmem] * len(operands),
        out_specs=[vmem] * len(out_shape) if many else vmem,
        scratch_shapes=scratch,
        compiler_params=pltpu.CompilerParams(
            collective_id=collective_id, has_side_effects=True, vmem_limit_bytes=VMEM_LIMIT
        ),
    )(*operands)


def shape(*dims):
    return jax.ShapeDtypeStruct(dims, BF16)


def slot_places(routes_local):
    rows = routes_local.shape[0]
    ids = jnp.arange(EXPERTS, dtype=jnp.int32)
    named = routes_local[:, :, None] == ids[None, None, :]
    chosen = jnp.any(named, axis=1).astype(BF16)
    order = jnp.arange(rows, dtype=jnp.int32)
    earlier = (order[:, None] > order[None, :]).astype(BF16)
    before = jnp.dot(earlier, chosen, preferred_element_type=F32)
    position = jnp.sum(jnp.where(named, before[:, None, :], 0.0), axis=2).astype(jnp.int32)
    return routes_local * CAP + position


def body(
    residual,
    queries,
    kv_cache,
    cache_lengths,
    out_proj,
    norm_gain,
    routes,
    gate_weights,
    expert_in,
    expert_out,
    shared_in,
    shared_out,
):
    rows = residual.shape[1]
    part = residual.shape[2]
    tp_count = lax.axis_size("tp")
    width = part * tp_count
    half_width = width // 2
    role, zh, y, z, x = places()
    head_count = queries.shape[2] // HD

    query_heads = queries.reshape(rows, head_count, HD)
    cache_rows = kv_cache.reshape(rows, L, 2 * HD)
    cache_keys = cache_rows[:, :, :HD]
    cache_values = cache_rows[:, :, HD:]
    scores = jnp.einsum("rhd,rld->rhl", query_heads, cache_keys, preferred_element_type=F32) * HD ** (-0.5)
    visible = jnp.arange(L, dtype=jnp.int32)[None, None, :] < cache_lengths.reshape(rows)[:, None, None]
    scores = jnp.where(visible, scores, -1e30)
    maximum = jnp.max(scores, axis=-1, keepdims=True)
    exponent = jnp.where(visible, jnp.exp(scores - maximum), 0.0)
    attn_weights = (exponent / jnp.sum(exponent, axis=-1, keepdims=True)).astype(BF16)
    context = jnp.einsum("rhl,rld->rhd", attn_weights, cache_values, preferred_element_type=F32).astype(BF16)
    context = context.reshape(rows, head_count * HD)
    attended = jnp.einsum("kd,rk->dr", out_proj, context, preferred_element_type=F32).astype(BF16)

    small_half = (part // 2, rows)
    hidden = call(
        hidden_kernel,
        1,
        shape(tp_count, part, rows),
        plane_sum_scratch(small_half) + plane_gather_scratch(),
        attended.reshape(tp_count, part, rows),
        residual.reshape(rows, part).T,
    )
    hidden_part = lax.dynamic_index_in_dim(hidden, z * 4 + x, 0, keepdims=False)
    hidden_wide = hidden.reshape(width, rows).astype(F32)
    mean_square = jnp.mean(hidden_wide * hidden_wide, axis=0, keepdims=True)
    normed = (hidden_wide * lax.rsqrt(mean_square + 1e-06) * norm_gain.astype(F32)[:, None]).astype(BF16)

    slot_index = slot_places(routes.reshape(rows, TOPK))
    gates = gate_weights.reshape(rows, TOPK)
    owners = jnp.arange(2, dtype=jnp.int32)[:, None] * 8 + zh * 4 + jnp.arange(4, dtype=jnp.int32)[None, :]
    inside = jnp.arange(UNIT, dtype=jnp.int32)
    same_ids = (owners.reshape(8)[:, None] * UNIT + inside[None, :]).reshape(8 * UNIT)
    cross_owner = flip(role, x % 2) * 8 + (1 - zh) * 4 + xor4(y, z)
    cross_ids = cross_owner * UNIT + inside
    cross_half = x // 2

    same_hit = same_ids[:, None, None] == slot_index[None, :, :]
    cross_hit = cross_ids[:, None, None] == slot_index[None, :, :]
    same_pick = jnp.any(same_hit, axis=2).astype(BF16)
    cross_pick = jnp.any(cross_hit, axis=2).astype(BF16)
    same_rows = jnp.einsum("sr,dr->sd", same_pick, normed, preferred_element_type=F32).astype(BF16)
    normed_half = lax.dynamic_slice_in_dim(normed, cross_half * half_width, half_width, 0)
    cross_rows = jnp.einsum("sr,dr->sd", cross_pick, normed_half, preferred_element_type=F32).astype(BF16)

    dma = pltpu.SemaphoreType.DMA
    got_same, got_cross = call(
        dispatch_kernel,
        2,
        [shape(2, 4, UNIT, width), shape(tp_count, UNIT, half_width)],
        [dma((1,)), dma((1,))] + column_scratch(UNIT, width) + plane_gather_scratch(),
        same_rows.reshape(2, 4, UNIT, width),
        cross_rows,
    )

    shared_pre = jnp.einsum("dr,gfd->rgf", normed, shared_in, preferred_element_type=F32)
    shared_act = (jax.nn.silu(shared_pre[:, 0]) * shared_pre[:, 1]).astype(BF16)
    shared_partial = jnp.einsum("fd,rf->dr", shared_out, shared_act, preferred_element_type=F32)

    hidden_units = expert_out.shape[1]
    w_in = expert_in.reshape(4 * hidden_units, width)
    w_out = expert_out.reshape(2 * hidden_units, width)

    def activate(pre):
        pre = pre.reshape(-1, 2, 2, hidden_units)
        act = jax.nn.silu(pre[:, :, 0]) * pre[:, :, 1]
        slot_expert = (jnp.arange(act.shape[0], dtype=jnp.int32) % UNIT) // CAP
        act = jnp.where(slot_expert[:, None, None] == jnp.arange(2, dtype=jnp.int32)[None, :, None], act, 0.0)
        return act.reshape(-1, 2 * hidden_units).astype(BF16)

    same_pre = jnp.einsum("sd,fd->sf", got_same.reshape(8 * UNIT, width), w_in, preferred_element_type=F32)
    cross_in = got_cross.reshape(4, 2, 2 * UNIT, half_width)
    cross_pre = sum(
        jnp.einsum(
            "sd,fd->sf",
            cross_in[:, h].reshape(8 * UNIT, half_width),
            w_in[:, h * half_width : (h + 1) * half_width],
            preferred_element_type=F32,
        )
        for h in range(2)
    )
    same_out = jnp.dot(activate(same_pre), w_out, preferred_element_type=F32).astype(BF16)
    cross_act = activate(cross_pre)
    cross_out = jnp.stack(
        [
            jnp.dot(cross_act, w_out[:, h * half_width : (h + 1) * half_width], preferred_element_type=F32)
            .astype(BF16)
            .reshape(4, 2 * UNIT, half_width)
            for h in range(2)
        ],
        axis=1,
    )

    back_same, back_cross, _ = call(
        return_kernel,
        3,
        [shape(2, 4, UNIT, width), shape(UNIT, half_width), shape(UNIT, half_width)],
        [dma((1,)), dma((1,))] + column_scratch(UNIT, width) + plane_sum_scratch((UNIT, half_width // 2)),
        same_out.reshape(2, 4, UNIT, width),
        cross_out.reshape(tp_count, UNIT, half_width),
    )

    def weigh(hit, table):
        weight = jnp.sum(jnp.where(hit, gates[None, :, :], 0.0), axis=2)
        high = weight.astype(BF16)
        low = (weight - high.astype(F32)).astype(BF16)
        return jnp.einsum("sd,sr->dr", table, high, preferred_element_type=F32) + jnp.einsum(
            "sd,sr->dr", table, low, preferred_element_type=F32
        )

    routed = weigh(same_hit, back_same.reshape(8 * UNIT, width))
    routed_cross = weigh(cross_hit, back_cross)
    halves = jnp.arange(2, dtype=jnp.int32)[:, None, None]
    branches = (shared_partial + routed).reshape(2, half_width, rows)
    branches = (branches + jnp.where(halves == cross_half, routed_cross[None], 0.0)).astype(BF16)

    layer_out = call(
        output_kernel,
        4,
        shape(part, rows),
        plane_sum_scratch(small_half),
        branches.reshape(tp_count, part, rows),
        hidden_part,
    )
    return layer_out.T.reshape(1, rows, part)


def solution(mesh):
    in_specs = (
        P("role", "grp", "tp"),
        P("role", "grp", "tp"),
        P("role", "grp", None, None),
        P("role", "grp"),
        P("tp", None),
        P(),
        P("role", "grp", None),
        P("role", "grp", None),
        P(("role", "grp"), None, "tp", None),
        P(("role", "grp"), "tp", None),
        P(None, "tp", None),
        P("tp", None),
    )
    out_specs = P("role", "grp", "tp")
    return jax.shard_map(body, mesh=mesh, in_specs=in_specs, out_specs=out_specs, check_vma=False)
```

time: 535 us -> 211 us (0.39); the launches traced: 525 us -> 209 us
  waiting for transfers between devices: 276 us -> 0 us
  blocking collectives: 175 us -> 0 us
  Pallas kernels: 0 us -> 154 us
  between operations: 13.6 us -> 0.3 us
  starting transfers between devices: 7.66 us -> 0 us
  local copies, waits for them, and re-layouts: 27.7 us -> 20.6 us
  matrix products: 19.9 us -> 25.6 us
    reduce_scatter x2 -> x0, waiting for transfers between devices: 157 us -> none  [the longest x1 78.9 us: body(): lax.psum_scatter(shared_partial + routed, 'tp', scatter_dimension=1, tile...]
    pallas_call x0 -> x4, Pallas kernels: none -> 154 us  [call(): pl.pallas_call(kernel, out_shape=out_shape, in_specs=[vmem] * len(operand...]
    all_to_all x1 -> x0, blocking collectives: 139 us -> none  [body(): lax.all_to_all(outgoing, ('role', 'grp'), split_axis=0, concat_axis=0, ti...]
    all_to_all x1 -> x0, waiting for transfers between devices: 119 us -> none  [body(): lax.all_to_all(produced, ('role', 'grp'), split_axis=0, concat_axis=0, ti...]
    all_gather x1 -> x0, blocking collectives: 36 us -> none  [body(): hidden = lax.all_gather(hidden_part, 'tp', axis=1, tiled=True)]
    gather x6 -> x0, local copies, waits for them, and re-layouts: 21.6 us -> none  [the longest x4 13.1 us: combine_slots(): slot_table[slot_index[:, choose]].astype(jnp.float32)]
    all_to_all x1 -> x0, starting transfers between devices: 7.44 us -> none  [body(): lax.all_to_all(produced, ('role', 'grp'), split_axis=0, concat_axis=0, ti...]
    unnamed x20 -> x33, local copies, waits for them, and re-layouts: 1 us -> 7.17 us
  transfers between devices with their start and end apart: 3 -> 0, of which waited for: 3 -> 0; matrix products, arithmetic and copies ran while one was open for 1% -> 0% of each run, Pallas kernels for 0% -> 0%
where the time goes in v1:
time: 211 us; the launch traced here: 209 us
  Pallas kernels  154 us (73%)
  matrix products  25.6 us (12%)
  local copies, waits for them, and re-layouts  20.6 us (10%)
  other arithmetic  8.36 us (4%)
    pallas_call x4, Pallas kernels, call(): pl.pallas_call(kernel, out_shape=out_shape, in_specs=[vmem] * len(operand...  154 us
    unnamed x33, local copies, waits for them, and re-layouts  7.17 us
    dot_general x1, matrix products, body(): jnp.einsum('sd,fd->sf', got_same.reshape(8 * UNIT, width), w_in, preferre...  4.84 us

profile of v1, /device:TPU:1, one launch (start us, length us, event | category | flops | bytes accessed | tf_op | source)
XLA Modules:
  0.0 208.6 jit_solution(6088747513700849136)
XLA Ops:
  0.0 0.0 copy-start
  0.0 0.8 copy.69
  0.9 0.1 fusion.43
  1.0 0.7 fusion.54
  1.7 0.1 compare_reduce_fusion.1
  1.8 0.9 reshape.204
  2.7 0.7 iota_compare_fusion.1
  3.4 1.6 fusion.65
  5.0 0.0 copy-start.9
  5.0 1.5 convolution_convert_fusion.5
  6.6 0.1 copy-done.9
  6.7 0.4 fusion.3
  7.1 0.0 copy-start.11
  7.1 1.3 copy.42
  8.4 0.0 copy-done.3
  8.4 1.2 copy-done.2
  9.6 31.6 %shard_map.118 = bf16[16,224,128]{2,1,0:T(8,128)(2,1)S(1)} custom-call(bf16[16,224,128]{2,1,0:T(8,128)(2,1)S(1)} %bitcast.135, bf16[224,128]{1,0:T(8,128)(2,1)S(1)} %bitcast.137), custom_call_target="tpu_custom_call" | custom-call | tf_op jit(solution)/shard_map/pallas_call | solution.py:407
  41.2 0.5 multiply_reduce_fusion
  41.7 0.0 copy-done.11
  41.7 0.5 fusion.9
  42.3 0.0 copy-start.6
  42.3 0.9 copy-done.6
  43.2 0.3 convolution_convert_fusion.4.cross
  43.5 0.1 add_multiply_fusion
  43.6 0.1 mul.111
  43.7 0.1 iota_add_fusion
  43.8 0.1 add.194
  43.8 0.1 compare_reduce_fusion
  44.0 0.0 slice-start
  44.0 3.8 %convolution_convert_fusion = bf16[384,3584]{1,0:T(8,128)(2,1)} fusion(pred[384,128]{1,0:T(8,128)(4,1)S(1)} %compare_reduce_fusion, bf16[3584,128]{1,0:T(8,128)(2,1)} %copy-done.6), kind=kOutput, calls=%fused_computation.3 | convolution fusion | flops 353697792 | bytes 3719168 | tf_op jit(solution)/shard_map/sr,dr->sd/dot_general | solution.py:498
  47.8 53.1 %shard_map.119 = (bf16[2,4,48,3584]{3,2,1,0:T(8,128)(2,1)S(1)}, bf16[16,48,1792]{2,1,0:T(8,128)(2,1)}) custom-call(bf16[2,4,48,3584]{3,2,1,0:T(8,128)(2,1)} %bitcast.141, bf16[48,1792]{1,0:T(8,128)(2,1)S(1)} %convolution_convert_fusion.4.cross), custom_call_target="tpu_custom_call" | custom-call | tf_op jit(solution)/shard_map/pallas_call | solution.py:407
  100.9 2.9 %fusion.63 = (bf16[4,1,96,1792]{3,2,1,0:T(8,128)(2,1)S(1)}, bf16[4,1,96,1792]{3,2,1,0:T(8,128)(2,1)S(1)}) fusion(bf16[4,2,96,1792]{3,2,1,0:T(8,128)(2,1)} %bitcast.145), kind=kLoop, calls=%fused_computation.108 | loop fusion | bytes 5505024 | tf_op jit(solution)/shard_map/slice | solution.py:532
  103.9 1.3 fusion.4
  105.1 2.3 %fusion.10 = f32[384,640]{1,0:T(8,128)} fusion(f32[384,640]{1,0:T(8,128)S(1)} %fusion.4, bf16[384,1792]{1,0:T(8,128)(2,1)S(1)} %bitcast.148, bf16[640,3584]{1,0:T(8,128)(2,1)S(1)} %bitcast.161), kind=kOutput, calls=%fused_computation.23 | convolution fusion | flops 881049600 | bytes 5636096 | tf_op jit(solution)/shard_map/sd,fd->sf/dot_general | solution.py:530
  107.4 2.5 %copy.45 = f32[384,640]{0,1:T(8,128)} copy(f32[384,640]{1,0:T(8,128)} %fusion.10) | data formatting | bytes 1966080 | tf_op jit(solution)/shard_map/add | solution.py:529
  109.9 1.4 fusion.64
  111.3 0.2 fusion.28
  111.5 0.3 copy-done.8
  111.8 0.9 convolution_convert_fusion.3
  112.7 0.9 convolution_convert_fusion.2
  113.7 1.8 pad_maximum_fusion
  115.5 0.9 copy-done.5
  116.4 4.8 %fusion.68 = f32[384,2,2,160]{0,3,2,1:T(8,128)S(1)} fusion(bf16[384,3584,1,1]{1,0,3,2:T(8,128)(2,1)S(1)} %bitcast.138, bf16[2,2,160,3584]{3,2,1,0:T(8,128)(2,1)} %param.20), kind=kOutput, calls=%fused_computation.111 | convolution fusion | flops 1761607680 | bytes 8323072 | tf_op jit(solution)/shard_map/sd,fd->sf/dot_general | solution.py:527
  121.3 3.2 %fusion.1 = bf16[384,3584]{1,0:T(8,128)(2,1)} fusion(bf16[2,160,3584]{2,1,0:T(8,128)(2,1)S(1)} %copy-done.8, f32[384,2,2,160]{0,3,2,1:T(8,128)S(1)} %fusion.68, pred[384,2]{0,1:T(4,128)(4,1)S(1)} %iota_compare_fusion.4), kind=kOutput, calls=%fused_computation.2 | convolution fusion | flops 883040256 | bytes 6030080 | tf_op jit(solution)/shard_map/dot_general | solution.py:538
  124.5 51.9 %shard_map.120 = (bf16[2,4,48,3584]{3,2,1,0:T(8,128)(2,1)S(1)}, bf16[48,1792]{1,0:T(8,128)(2,1)S(1)}, bf16[48,1792]{1,0:T(8,128)(2,1)}) custom-call(bf16[2,4,48,3584]{3,2,1,0:T(8,128)(2,1)} %bitcast.140, bf16[16,48,1792]{2,1,0:T(8,128)(2,1)} %bitcast.139), custom_call_target="tpu_custom_call" | custom-call | tf_op jit(solution)/shard_map/pallas_call | solution.py:407
  176.4 0.1 fusion.39
  176.5 0.3 fusion.51
  176.8 0.3 convolution_add_fusion.1
  177.2 1.4 broadcast_in_dim.142
  178.5 0.1 fusion.21
  178.7 0.7 fusion.45
  179.4 0.0 copy-done
  179.4 0.5 copy-done.7
  179.9 0.8 fusion.19
  180.6 0.5 copy-done.10
  181.1 0.4 convolution_bitcast_fusion.1
  181.6 2.0 fusion.2
  183.5 2.7 %copy.50 = f32[3584,128]{1,0:T(8,128)} copy(f32[3584,128]{0,1:T(8,128)} %fusion.2) | data formatting | bytes 3670016 | tf_op jit(solution)/shard_map/add | solution.py:570
  186.3 0.1 broadcast_in_dim.137
  186.3 0.1 broadcast_in_dim.138
  186.4 3.3 %add_convert_fusion.part = bf16[16,224,128]{2,1,0:T(8,128)(2,1)} fusion(f32[16,224,128]{2,1,0:T(8,128)} %bitcast.142, f32[16,224,128]{2,1,0:T(8,128)} %bitcast.143, pred[16]{0:T(512)(128)(4,1)S(1)} %broadcast_in_dim.138), kind=kLoop, calls=%fused_computation.21 | loop fusion | flops 1376256 | bytes 4587536 | tf_op jit(solution)/shard_map/convert_element_type | solution.py:571
  189.7 1.2 copy-done.1
  190.9 17.0 %shard_map.121 = bf16[224,128]{1,0:T(8,128)(2,1)S(1)} custom-call(bf16[16,224,128]{2,1,0:T(8,128)(2,1)S(1)} %copy-done.1, bf16[224,128]{1,0:T(8,128)(2,1)S(1)} %dynamic-slice_bitcast_fusion.hidden), custom_call_target="tpu_custom_call" | custom-call | tf_op jit(solution)/shard_map/pallas_call | solution.py:407
  207.9 0.6 copy.72
  (26 shorter events, 0.1 us)
Async XLA Ops:
  0.0 179.4 %copy-start = (bf16[2,160,3584]{2,1,0:T(8,128)(2,1)S(1)}, bf16[2,160,3584]{2,1,0:T(8,128)(2,1)}, u32[]{:S(2)}) copy-start(bf16[2,160,3584]{2,1,0:T(8,128)(2,1)} %param.22) | copy-start | bytes 6881284
  5.0 1.7 copy-start.9
  6.7 1.7 copy-start.3
  7.1 34.6 %copy-start.11 = (bf16[3584]{0:T(1024)(128)(2,1)S(1)}, bf16[3584]{0:T(1024)(128)(2,1)}, u32[]{:S(2)}) copy-start(bf16[3584]{0:T(1024)(128)(2,1)} %param.17) | copy-start | bytes 21508
  8.4 1.2 copy-start.2
  42.3 1.0 copy-start.6
  44.0 59.9 %slice-start = ((s8[4587520]{0:T(1024)(128)(4,1)}), s8[4194304]{0:T(1024)(128)(4,1)S(1)}, s32[]{:S(2)}) async-start(s8[4587520]{0:T(1024)(128)(4,1)} %bitcast.158), calls=%async_computation | async-start | bytes 8388608
  47.8 56.1 %slice-start.1 = ((s8[4587520]{0:T(1024)(128)(4,1)}), s8[393216]{0:T(1024)(128)(4,1)S(1)}, s32[]{:S(2)}) async-start(s8[4587520]{0:T(1024)(128)(4,1)} %bitcast.158), calls=%async_computation.1 | async-start | bytes 786432
  100.9 2.9 %copy-start.4 = (bf16[2,4,48,3584]{3,2,1,0:T(8,128)(2,1)}, bf16[2,4,48,3584]{3,2,1,0:T(8,128)(2,1)S(1)}, u32[]{:S(2)}) copy-start(bf16[2,4,48,3584]{3,2,1,0:T(8,128)(2,1)S(1)} %get-tuple-element.9) | copy-start | bytes 8257540
  109.9 1.9 copy-start.8
  113.6 2.8 %copy-start.5 = (bf16[2,4,48,3584]{3,2,1,0:T(8,128)(2,1)S(1)}, bf16[2,4,48,3584]{3,2,1,0:T(8,128)(2,1)}, u32[]{:S(2)}) copy-start(bf16[2,4,48,3584]{3,2,1,0:T(8,128)(2,1)} %copy-done.4) | copy-start | bytes 8257540
  124.5 51.9 %copy-start.12 = (f32[1,128,3]{1,0,2:T(1,128)S(1)}, f32[1,128,3]{1,0,2:T(1,128)}, u32[]{:S(2)}) copy-start(f32[1,128,3]{1,0,2:T(1,128)} %param.19) | copy-start | bytes 4612
  178.7 1.2 copy-start.7
  179.9 1.3 copy-start.10
  189.7 1.2 copy-start.1

commit v2 on v0

v2 whole, which is shorter than its diff:
```python
import functools

import jax
import jax.numpy as jnp
from jax import lax
from jax.experimental import pallas as pl
from jax.experimental.pallas import tpu as pltpu
from jax.sharding import PartitionSpec as P

HD = 128
EXPERTS = 32
TOPK = 3
L = 16
CAP = 24
UNIT = 2 * CAP
MESH = pl.DeviceIdType.MESH
BF16 = jnp.bfloat16
F32 = jnp.float32
VMEM_LIMIT = 50 * 1024 * 1024


def places():
    role, grp, tp = lax.axis_index("role"), lax.axis_index("grp"), lax.axis_index("tp")
    return role, grp // 4, grp % 4, tp // 4, tp % 4


def flip(a, b):
    return (a + b) % 2


def xor4(a, b):
    return 2 * flip(a // 2, b // 2) + flip(a % 2, b % 2)


def z_mates(z):
    return {1: xor4(z, 1), 2: (z + 2) % 4, 3: 3 - z}


def device(role, zh, y, z, x):
    return {"role": role, "grp": zh * 4 + y, "tp": z * 4 + x}


def partners(role, zh, y, z, x):
    there = (flip(role, x % 2), 1 - zh)
    return device(*there, xor4(y, z), 3 - z, x), device(*there, xor4(y, 3 - z), 3 - z, x)


def plane_mates(role, zh, y, z, x):
    mates = [device(role, zh, y, z, (x + 1) % 4), device(role, zh, y, z, (x + 3) % 4)]
    return mates + [device(role, zh, y, one, x) for one in z_mates(z).values()]


def column_mates(role, zh, y, z, x):
    mates = [device(one, zh, (y + step) % 4, z, x) for step in (1, 2, 3) for one in (0, 1)]
    return mates + [device(1 - role, zh, y, z, x)]


def send(src, dst, send_sem, recv_sem, to):
    copy = pltpu.make_async_remote_copy(
        src_ref=src, dst_ref=dst, send_sem=send_sem, recv_sem=recv_sem, device_id=to, device_id_type=MESH
    )
    copy.start()
    return copy


class PlaneSum:
    def __init__(self, here, part, half, rx1, tx, rx2, zt, zrx, s1, r1, s2, r2, zs, zr, own_first=False):
        self.here, self.part, self.half = here, part, half
        self.rx1, self.tx, self.rx2, self.zt, self.zrx = rx1, tx, rx2, zt, zrx
        self.s1, self.r1, self.s2, self.r2, self.zs, self.zr = s1, r1, s2, r2, zs, zr
        role, zh, y, z, x = here
        mates = z_mates(z)
        self.order = [z, mates[1], mates[3], mates[2]] if own_first else [mates[2], mates[3], mates[1], z]
        self.own = 0 if own_first else 3
        self.zslot = {i: n for n, i in enumerate(i for i in range(4) if i != self.own)}
        self.right, self.left = (x + 1) % 4, (x + 3) % 4
        self.to_right = device(role, zh, y, z, self.right)
        self.to_left = device(role, zh, y, z, self.left)
        self.copies = []
        self.first, self.second, self.zcopies = {}, {}, {}

    def begin(self, i):
        x = self.here[4]
        far = (x + 2) % 4
        base = self.order[i] * 4
        for d, (to, near) in enumerate(((self.to_right, self.right), (self.to_left, self.left))):
            self.first[i, d] = send(
                self.half(self.part, base + far, d), self.rx1.at[i, d], self.s1.at[i, d], self.r1.at[i, d], to
            )
            self.second[i, d, 1 - d] = send(
                self.half(self.part, base + near, 1 - d),
                self.rx2.at[i, d, 1 - d],
                self.s2.at[i, d, 1 - d],
                self.r2.at[i, d, 1 - d],
                to,
            )

    def middle(self, i):
        base = self.order[i] * 4
        for d, (to, near) in enumerate(((self.to_right, self.right), (self.to_left, self.left))):
            self.first[i, d].wait_recv()
            own = self.half(self.part, base + near, d)[...]
            self.tx[i, d] = (self.rx1[i, d].astype(F32) + own.astype(F32)).astype(BF16)
            self.second[i, d, d] = send(
                self.tx.at[i, d], self.rx2.at[i, d, d], self.s2.at[i, d, d], self.r2.at[i, d, d], to
            )

    def line(self, i, h):
        x = self.here[4]
        own = self.half(self.part, self.order[i] * 4 + x, h)[...].astype(F32)
        return own + self.rx2[i, 0, h].astype(F32) + self.rx2[i, 1, h].astype(F32)

    def end(self, i):
        role, zh, y, z, x = self.here
        for d in range(2):
            for h in range(2):
                self.second[i, d, h].wait_recv()
        if i == self.own:
            return
        n = self.zslot[i]
        for h in range(2):
            self.zt[n, h] = self.line(i, h).astype(BF16)
            self.zcopies[n, h] = send(
                self.zt.at[n, h],
                self.zrx.at[n, h],
                self.zs.at[n, h],
                self.zr.at[n, h],
                device(role, zh, y, self.order[i], x),
            )

    def total(self, h):
        value = self.line(self.own, h)
        for i in range(3):
            self.zcopies[i, h].wait_recv()
            value = value + self.zrx[i, h].astype(F32)
        return value

    def drain(self):
        for copy in list(self.first.values()) + list(self.second.values()) + list(self.zcopies.values()):
            copy.wait_send()

    def whole(self, between=lambda: None):
        for i in range(4):
            self.begin(i)
        self.middle(0)
        self.middle(1)
        between()
        self.end(0)
        self.middle(2)
        self.end(1)
        self.middle(3)
        self.end(2)
        self.end(3)


def plane_sum_scratch(half):
    dma = pltpu.SemaphoreType.DMA
    return [
        pltpu.VMEM((4, 2) + half, BF16),
        pltpu.VMEM((4, 2) + half, BF16),
        pltpu.VMEM((4, 2, 2) + half, BF16),
        pltpu.VMEM((3, 2) + half, BF16),
        pltpu.VMEM((3, 2) + half, BF16),
        dma((4, 2)),
        dma((4, 2)),
        dma((4, 2, 2)),
        dma((4, 2, 2)),
        dma((3, 2)),
        dma((3, 2)),
    ]


class PlaneGather:
    def __init__(self, here, out, half, zs, zr, xs, xr, fs, fr):
        self.here, self.out, self.half = here, out, half
        self.zs, self.zr, self.xs, self.xr, self.fs, self.fr = zs, zr, xs, xr, fs, fr
        role, zh, y, z, x = here
        mates = z_mates(z)
        self.order = [z, mates[1], mates[3], mates[2]]
        self.to_right = device(role, zh, y, z, (x + 1) % 4)
        self.to_left = device(role, zh, y, z, (x + 3) % 4)
        self.zcopies, self.near, self.far = {}, {}, {}

    def begin(self):
        role, zh, y, z, x = self.here
        mine = z * 4 + x
        self.start(0)
        for m in (1, 2, 3):
            for h in range(2):
                block = self.half(self.out, mine, h)
                self.zcopies[m, h] = send(
                    block, block, self.zs.at[m - 1, h], self.zr.at[m - 1, h], device(role, zh, y, self.order[m], x)
                )

    def start(self, i):
        x = self.here[4]
        slot = self.order[i] * 4 + x
        if i > 0:
            for h in range(2):
                self.zcopies[i, h].wait_recv()
        for h in range(2):
            for d, to in enumerate((self.to_right, self.to_left)):
                block = self.half(self.out, slot, h if d == 0 else 1 - h)
                k = h if d == 0 else 1 - h
                self.near[i, d, k] = send(block, block, self.xs.at[i, d, k], self.xr.at[i, d, k], to)

    def pass_on(self, i):
        x = self.here[4]
        base = self.order[i] * 4
        for d, (to, slot) in enumerate(((self.to_right, (x + 3) % 4), (self.to_left, (x + 1) % 4))):
            self.near[i, d, d].wait_recv()
            block = self.half(self.out, base + slot, d)
            self.far[i, d] = send(block, block, self.fs.at[i, d], self.fr.at[i, d], to)

    def complete(self, i):
        for d in range(2):
            self.near[i, d, 1 - d].wait_recv()
            self.far[i, d].wait_recv()

    def finish(self):
        for copies in (self.zcopies, self.near, self.far):
            for copy in copies.values():
                copy.wait_send()

    def whole(self, between=lambda: None):
        self.begin()
        self.pass_on(0)
        self.start(1)
        between()
        self.start(2)
        self.pass_on(1)
        self.start(3)
        self.pass_on(2)
        self.pass_on(3)
        for i in range(4):
            self.complete(i)
        self.finish()


def plane_gather_scratch():
    dma = pltpu.SemaphoreType.DMA
    return [dma((3, 2)), dma((3, 2)), dma((4, 2, 2)), dma((4, 2, 2)), dma((4, 2)), dma((4, 2))]


def flat_half(ref, slot, h):
    rows = ref.shape[0] // 32
    return ref.at[pl.ds(pl.multiple_of((2 * slot + h) * rows, 16), rows), :]


def lane_half(ref, slot, h):
    width = ref.shape[2] // 2
    return ref.at[slot, :, pl.ds(h * width, width)]


def dot(a, b):
    return jnp.dot(a, b, preferred_element_type=F32)


def dot_rows(a, b):
    return lax.dot_general(a, b, (((1,), (1,)), ((), ())), preferred_element_type=F32)


def split(value):
    high = value.astype(BF16)
    return high, (value - high.astype(F32)).astype(BF16)


def slot_rows(routes):
    count = routes.shape[1]
    ids = lax.broadcasted_iota(jnp.int32, (EXPERTS, count), 0)
    named = [ids == routes[k : k + 1, :] for k in range(TOPK)]
    chosen = jnp.where(named[0] | named[1] | named[2], 1.0, 0.0).astype(BF16)
    earlier = lax.broadcasted_iota(jnp.int32, (count, count), 0) < lax.broadcasted_iota(jnp.int32, (count, count), 1)
    before = dot(chosen, jnp.where(earlier, 1.0, 0.0).astype(BF16))
    place = [jnp.sum(jnp.where(one, before, 0.0), axis=0, keepdims=True).astype(jnp.int32) for one in named]
    return [routes[k : k + 1, :] * CAP + place[k] for k in range(TOPK)]


def unit_hits(slots, owner):
    ids = lax.broadcasted_iota(jnp.int32, (UNIT, slots[0].shape[1]), 0) + owner * UNIT
    return [ids == one for one in slots]


def layer_kernel(names, part, resid, gain, routes, gates, w_in, w_out, s_in, s_out, out, *scratch):
    ref = dict(zip(names, scratch))
    here = places()
    role, zh, y, z, x = here
    mine = z * 4 + x
    rows = routes.shape[1]
    width = gain.shape[1]
    half = width // 2
    units = w_in.shape[2]
    to, source = partners(*here)

    barrier = pltpu.get_barrier_semaphore()
    mates = plane_mates(*here) + column_mates(*here) + [to, source]
    for one in mates:
        pl.semaphore_signal(barrier, inc=1, device_id=one, device_id_type=MESH)

    loads = []
    for j in range(2):
        loads.append((w_in.at[j, 0], ref["gate"].at[pl.ds(j * units, units), :]))
        loads.append((w_in.at[j, 1], ref["up"].at[pl.ds(j * units, units), :]))
        loads.append((w_out.at[j], ref["down"].at[pl.ds(j * units, units), :]))
        loads.append((s_in.at[j], ref["shared_in"].at[j]))
    loads.append((s_out, ref["shared_out"]))
    loads = [pltpu.make_async_copy(a, b, ref["load"].at[i]) for i, (a, b) in enumerate(loads)]
    for one in loads:
        one.start()

    slots = slot_rows(routes[...])
    gate_rows = gates[...]

    def pick(owner):
        hits = unit_hits(slots, owner)
        return jnp.where(hits[0] | hits[1] | hits[2], 1.0, 0.0).astype(BF16)

    def weigh(owner):
        hits = unit_hits(slots, owner)
        return sum(jnp.where(hits[k], gate_rows[k : k + 1, :], 0.0) for k in range(TOPK))

    def owner_of(q, yo):
        return q * 8 + zh * 4 + yo

    cross_owner = flip(role, x % 2) * 8 + (1 - zh) * 4 + xor4(y, z)
    cross_half = x // 2

    pl.semaphore_wait(barrier, len(mates))
    first = PlaneSum(here, part, flat_half, *[ref[f"a{i}"] for i in range(11)])
    first.whole()
    hidden = ref["hidden"]
    step = resid.shape[0] // 2
    for h in range(2):
        value = first.total(h) + resid[pl.ds(h * step, step), :].astype(F32)
        flat_half(hidden, mine, h)[...] = value.astype(BF16)
    PlaneGather(here, hidden, flat_half, *[ref[f"b{i}"] for i in range(6)]).whole()

    normed = ref["normed"]
    tile = 256
    square = jnp.zeros((rows, 1), F32)
    for i in range(width // tile):
        wide = hidden[pl.ds(i * tile, tile), :].astype(F32).T
        square = square + jnp.sum(wide * wide, axis=1, keepdims=True)
        normed[:, pl.ds(i * tile, tile)] = wide.astype(BF16)
    scale = lax.rsqrt(square / width + 1e-06)
    for i in range(width // tile):
        at = pl.ds(i * tile, tile)
        normed[:, at] = (normed[:, at].astype(F32) * scale * gain[:, at]).astype(BF16)

    chosen = pick(cross_owner)
    got_cross = ref["got_cross"]
    swaps = []
    for h in range(2):
        at = pl.ds(h * (half // 2), half // 2)
        from_at = pl.ds(pl.multiple_of(cross_half * half + h * (half // 2), 128), half // 2)
        ref["cross"][:, at] = dot(chosen, normed[:, from_at]).astype(BF16)
        swaps.append(
            send(
                ref["cross"].at[:, at],
                got_cross.at[(3 - z) * 4 + x, :, at],
                ref["swap"].at[0, h],
                ref["swap"].at[1, h],
                to,
            )
        )
    same, got_same, back_same = ref["same"], ref["got_same"], ref["back_same"]
    sent = []

    def pick_into(target, owner):
        chosen = pick(owner)
        for h in range(4):
            at = pl.ds(h * (width // 4), width // 4)
            target[:, at] = dot(chosen, normed[:, at]).astype(BF16)

    for d in (2, 1, 3):
        yo = (y + d) % 4
        for q in range(2):
            pick_into(same.at[q, yo], owner_of(q, yo))
            sent.append(
                send(
                    same.at[q, yo],
                    got_same.at[role, y],
                    ref["near"].at[0, d - 1, q],
                    ref["near"].at[1, d - 1, role],
                    device(q, zh, yo, z, x),
                )
            )
    pick_into(same.at[1 - role, y], owner_of(1 - role, y))
    core = send(
        same.at[1 - role, y], got_same.at[role, y], ref["core"].at[0], ref["core"].at[1], device(1 - role, zh, y, z, x)
    )
    pick_into(got_same.at[role, y], owner_of(role, y))

    for one in loads:
        one.wait()

    for q in range(2):
        for yo in range(4):
            at = pl.ds((q * 4 + yo) * UNIT, UNIT)
            ref["weights"][at, :] = weigh(owner_of(q, yo))
    ref["gate_high"][...], ref["gate_low"][...] = split(ref["weights"][...].T)
    ref["cross_high"][...], ref["cross_low"][...] = split(weigh(cross_owner).T)
    pre = [dot_rows(normed[...], ref["shared_in"][g]) for g in range(2)]
    ref["shared_act"][...] = (jax.nn.silu(pre[0]) * pre[1]).astype(BF16)

    both = 2 * UNIT
    inner = (lax.broadcasted_iota(jnp.int32, (both, 2 * units), 0) % UNIT) >= CAP
    second = lax.broadcasted_iota(jnp.int32, (both, 2 * units), 1) >= units
    own_expert = jnp.logical_not(jnp.logical_xor(inner, second))

    def experts(load, store):
        at = [pl.ds(h * half, half) for h in range(2)]
        found = [load(h) for h in range(2)]
        gate_pre = sum(dot_rows(found[h], ref["gate"][:, at[h]]) for h in range(2))
        up_pre = sum(dot_rows(found[h], ref["up"][:, at[h]]) for h in range(2))
        act = jnp.where(own_expert, jax.nn.silu(gate_pre) * up_pre, 0.0).astype(BF16)
        for h in range(2):
            for c in range(2):
                columns = pl.ds(h * half + c * (half // 2), half // 2)
                result = dot(act, ref["down"][:, columns]).astype(BF16)
                store(h, c, result.reshape(2, UNIT, half // 2))

    made_same, made_cross = ref["made_same"], ref["made_cross"]

    def same_experts(yo):
        def load(h):
            return got_same[:, yo, :, pl.ds(h * half, half)].reshape(both, half)

        def store(h, c, value):
            made_same[:, yo, :, pl.ds(h * half + c * (half // 2), half // 2)] = value

        experts(load, store)

    def cross_experts(zz):
        def load(h):
            return got_cross[pl.ds(zz * 4 + 2 * h, 2)].reshape(both, half)

        def store(h, c, value):
            made_cross[pl.ds(zz * 4 + 2 * h, 2), :, pl.ds(c * (half // 2), half // 2)] = value

        experts(load, store)

    def arrived(block, sem):
        pltpu.make_async_copy(block, block, sem).wait()

    def column_step(d):
        yo = (y + 4 - d) % 4
        for q in range(2):
            arrived(got_same.at[q, yo], ref["near"].at[1, d - 1, q])
        same_experts(yo)
        for q in range(2):
            sent.append(
                send(
                    made_same.at[q, yo],
                    back_same.at[role, y],
                    ref["back"].at[0, d - 1, q],
                    ref["back"].at[1, d - 1, role],
                    device(q, zh, yo, z, x),
                )
            )

    core.wait_recv()
    same_experts(y)
    core_back = send(
        made_same.at[1 - role, y],
        back_same.at[role, y],
        ref["core"].at[2],
        ref["core"].at[3],
        device(1 - role, zh, y, z, x),
    )
    own_back = pltpu.make_async_copy(made_same.at[role, y], back_same.at[role, y], ref["core"].at[4])
    own_back.start()

    gather = PlaneGather(here, got_cross, lane_half, *[ref[f"c{i}"] for i in range(6)])
    sums = PlaneSum(here, made_cross, lane_half, *[ref[f"d{i}"] for i in range(11)], own_first=True)

    def cross_step(i):
        gather.complete(i)
        cross_experts(gather.order[i])
        sums.begin(i)

    for one in swaps:
        one.wait_recv()
    gather.begin()
    gather.pass_on(0)
    gather.start(1)
    gather.pass_on(1)
    column_step(1)
    gather.start(2)
    cross_step(0)
    gather.pass_on(2)
    gather.start(3)
    column_step(3)
    gather.pass_on(3)
    cross_step(1)
    sums.middle(0)
    column_step(2)
    sums.end(0)
    cross_step(2)
    sums.middle(1)
    sums.end(1)
    cross_step(3)
    sums.middle(2)
    sums.end(2)
    sums.middle(3)
    sums.end(3)
    for h in range(2):
        at = pl.ds(h * (half // 2), half // 2)
        ref["done"][:, at] = sums.total(h).astype(BF16)
        swaps.append(
            send(ref["done"].at[:, at], ref["back_cross"].at[:, at], ref["swap"].at[2, h], ref["swap"].at[3, h], source)
        )

    core_back.wait_recv()
    own_back.wait()
    for d in (1, 3, 2):
        for q in range(2):
            arrived(back_same.at[q, (y + d) % 4], ref["back"].at[1, d - 1, q])
    swaps[2].wait_recv()
    swaps[3].wait_recv()
    branches = ref["branches"]
    per_half = half // tile
    for i in range(width // tile):
        at = pl.ds(i * tile, tile)
        table = back_same[:, :, :, at].reshape(8 * UNIT, tile)
        value = dot(ref["shared_act"][...], ref["shared_out"][:, at])
        value = value + dot(ref["gate_high"][...], table) + dot(ref["gate_low"][...], table)
        table = ref["back_cross"][:, pl.ds((i % per_half) * tile, tile)]
        routed = dot(ref["cross_high"][...], table) + dot(ref["cross_low"][...], table)
        value = value + jnp.where(cross_half == i // per_half, routed, 0.0)
        branches[at, :] = value.T.astype(BF16)

    last = PlaneSum(here, branches, flat_half, *[ref[f"e{i}"] for i in range(11)])
    last.whole()
    for h in range(2):
        value = last.total(h) + flat_half(hidden, mine, h)[...].astype(F32)
        out[pl.ds(h * step, step), :] = value.astype(BF16)

    for one in (first, sums, last):
        one.drain()
    gather.finish()
    for one in sent + swaps + [core, core_back]:
        one.wait_send()


def layer_scratch(rows, width, units, tp_count):
    half, part = width // 2, width // tp_count
    small, large = (part // 2, rows), (UNIT, half // 2)
    dma, vmem = pltpu.SemaphoreType.DMA, pltpu.VMEM
    named = {
        "gate": vmem((2 * units, width), BF16),
        "up": vmem((2 * units, width), BF16),
        "down": vmem((2 * units, width), BF16),
        "shared_in": vmem((2, units, width), BF16),
        "shared_out": vmem((units, width), BF16),
        "load": dma((9,)),
        "hidden": vmem((width, rows), BF16),
        "normed": vmem((rows, width), BF16),
        "cross": vmem((UNIT, half), BF16),
        "got_cross": vmem((tp_count, UNIT, half), BF16),
        "made_cross": vmem((tp_count, UNIT, half), BF16),
        "done": vmem((UNIT, half), BF16),
        "back_cross": vmem((UNIT, half), BF16),
        "same": vmem((2, 4, UNIT, width), BF16),
        "got_same": vmem((2, 4, UNIT, width), BF16),
        "made_same": vmem((2, 4, UNIT, width), BF16),
        "back_same": vmem((2, 4, UNIT, width), BF16),
        "weights": vmem((8 * UNIT, rows), F32),
        "gate_high": vmem((rows, 8 * UNIT), BF16),
        "gate_low": vmem((rows, 8 * UNIT), BF16),
        "cross_high": vmem((rows, UNIT), BF16),
        "cross_low": vmem((rows, UNIT), BF16),
        "shared_act": vmem((rows, units), BF16),
        "branches": vmem((width, rows), BF16),
        "swap": dma((4, 2)),
        "near": dma((2, 3, 2)),
        "back": dma((2, 3, 2)),
        "core": dma((5,)),
    }
    for letter, some in (
        ("a", plane_sum_scratch(small)),
        ("b", plane_gather_scratch()),
        ("c", plane_gather_scratch()),
        ("d", plane_sum_scratch(large)),
        ("e", plane_sum_scratch(small)),
    ):
        named.update({f"{letter}{i}": one for i, one in enumerate(some)})
    return list(named), list(named.values())


def body(
    residual,
    queries,
    kv_cache,
    cache_lengths,
    out_proj,
    norm_gain,
    routes,
    gate_weights,
    expert_in,
    expert_out,
    shared_in,
    shared_out,
):
    rows = residual.shape[1]
    part = residual.shape[2]
    tp_count = lax.axis_size("tp")
    width = part * tp_count
    head_count = queries.shape[2] // HD

    query_heads = queries.reshape(rows, head_count, HD)
    cache_rows = kv_cache.reshape(rows, L, 2 * HD)
    cache_keys = cache_rows[:, :, :HD]
    cache_values = cache_rows[:, :, HD:]
    scores = jnp.einsum("rhd,rld->rhl", query_heads, cache_keys, preferred_element_type=F32) * HD ** (-0.5)
    visible = jnp.arange(L, dtype=jnp.int32)[None, None, :] < cache_lengths.reshape(rows)[:, None, None]
    scores = jnp.where(visible, scores, -1e30)
    maximum = jnp.max(scores, axis=-1, keepdims=True)
    exponent = jnp.where(visible, jnp.exp(scores - maximum), 0.0)
    attn_weights = (exponent / jnp.sum(exponent, axis=-1, keepdims=True)).astype(BF16)
    context = jnp.einsum("rhl,rld->rhd", attn_weights, cache_values, preferred_element_type=F32).astype(BF16)
    context = context.reshape(rows, head_count * HD)
    attended = jnp.einsum("kd,rk->dr", out_proj, context, preferred_element_type=F32).astype(BF16)

    names, scratch = layer_scratch(rows, width, expert_out.shape[1], tp_count)
    vmem, hbm = pl.BlockSpec(memory_space=pltpu.VMEM), pl.BlockSpec(memory_space=pl.ANY)
    layer_out = pl.pallas_call(
        functools.partial(layer_kernel, names),
        out_shape=jax.ShapeDtypeStruct((part, rows), BF16),
        in_specs=[vmem] * 5 + [hbm] * 4,
        out_specs=vmem,
        scratch_shapes=scratch,
        compiler_params=pltpu.CompilerParams(collective_id=1, has_side_effects=True, vmem_limit_bytes=VMEM_LIMIT),
    )(
        attended,
        residual.reshape(rows, part).T,
        norm_gain.astype(F32).reshape(1, width),
        routes.reshape(rows, TOPK).T,
        gate_weights.reshape(rows, TOPK).T,
        expert_in,
        expert_out,
        shared_in,
        shared_out,
    )
    return layer_out.T.reshape(1, rows, part)


def solution(mesh):
    in_specs = (
        P("role", "grp", "tp"),
        P("role", "grp", "tp"),
        P("role", "grp", None, None),
        P("role", "grp"),
        P("tp", None),
        P(),
        P("role", "grp", None),
        P("role", "grp", None),
        P(("role", "grp"), None, "tp", None),
        P(("role", "grp"), "tp", None),
        P(None, "tp", None),
        P("tp", None),
    )
    out_specs = P("role", "grp", "tp")
    return jax.shard_map(body, mesh=mesh, in_specs=in_specs, out_specs=out_specs, check_vma=False)
```

time: 535 us -> 162 us (0.30); the launches traced: 525 us -> 160 us
  waiting for transfers between devices: 276 us -> 0 us
  blocking collectives: 175 us -> 0 us
  Pallas kernels: 0 us -> 154 us
  local copies, waits for them, and re-layouts: 27.7 us -> 2 us
  matrix products: 19.9 us -> 2.8 us
  between operations: 13.6 us -> 0.14 us
  starting transfers between devices: 7.66 us -> 0 us
    reduce_scatter x2 -> x0, waiting for transfers between devices: 157 us -> none  [the longest x1 78.9 us: body(): lax.psum_scatter(shared_partial + routed, 'tp', scatter_dimension=1, tile...]
    pallas_call x0 -> x1, Pallas kernels: none -> 154 us  [body(): pl.pallas_call(functools.partial(layer_kernel, names), out_shape=jax.Shap...]
    all_to_all x1 -> x0, blocking collectives: 139 us -> none  [body(): lax.all_to_all(outgoing, ('role', 'grp'), split_axis=0, concat_axis=0, ti...]
    all_to_all x1 -> x0, waiting for transfers between devices: 119 us -> none  [body(): lax.all_to_all(produced, ('role', 'grp'), split_axis=0, concat_axis=0, ti...]
    all_gather x1 -> x0, blocking collectives: 36 us -> none  [body(): hidden = lax.all_gather(hidden_part, 'tp', axis=1, tiled=True)]
    gather x6 -> x0, local copies, waits for them, and re-layouts: 21.6 us -> none  [the longest x4 13.1 us: combine_slots(): slot_table[slot_index[:, choose]].astype(jnp.float32)]
    dot_general x6 -> x1, matrix products: 16.3 us -> 0.86 us  [body(): jnp.einsum('kd,rk->dr', out_proj, context, preferred_element_type=F32)]
    all_to_all x1 -> x0, starting transfers between devices: 7.44 us -> none  [body(): lax.all_to_all(produced, ('role', 'grp'), split_axis=0, concat_axis=0, ti...]
  transfers between devices with their start and end apart: 3 -> 0, of which waited for: 3 -> 0; matrix products, arithmetic and copies ran while one was open for 1% -> 0% of each run, Pallas kernels for 0% -> 0%
where the time goes in v2:
time: 162 us; the launch traced here: 160 us
  Pallas kernels  154 us (95%)
  matrix products  2.8 us (2%)
  local copies, waits for them, and re-layouts  2 us (1%)
    pallas_call x1, Pallas kernels, body(): pl.pallas_call(functools.partial(layer_kernel, names), out_shape=jax.Shap...  154 us

profile of v2, /device:TPU:1, one launch (start us, length us, event | category | flops | bytes accessed | tf_op | source)
XLA Modules:
  0.0 160.1 jit_solution(4410878239956204639)
XLA Ops:
  0.0 0.0 copy-start
  0.0 0.0 copy-start.6
  0.0 1.0 reshape.52
  1.0 0.7 iota_compare_fusion
  1.8 1.6 fusion.11
  3.4 0.0 copy-done.6
  3.4 0.3 convolution_convert_fusion.1
  3.7 0.0 copy-start.3
  3.7 0.0 copy-start.4
  3.7 0.0 copy-start.5
  3.8 0.0 copy-start.1
  3.8 0.0 copy-start.2
  3.8 0.0 copy-done
  3.8 0.9 fusion.1.part
  4.7 0.0 copy-done.3
  4.7 0.0 copy-done.4
  4.7 0.0 copy-done.5
  4.7 0.3 copy-done.1
  5.0 0.0 copy-done.2
  5.0 154.4 %shard_map.118 = bf16[224,128]{1,0:T(8,128)(2,1)S(1)} custom-call(bf16[3584,128]{1,0:T(8,128)(2,1)S(1)} %fusion.1.part, bf16[224,128]{1,0:T(8,128)(2,1)S(1)} %bitcast.27, f32[1,3584]{1,0:T(1,128)S(1)} %reshape.62.gain, s32[3,128]{1,0:T(4,128)S(1)} %bitcast.29, f32[3,128]{1,0:T(4,128)S(1)} %bitcast.28, bf16[2,2,160,3584]{3,2,1,0:T(8,128)(2,1)} %w_in.1, ...), custom_call_target="tpu_custom_call" | custom-call | tf_op jit(solution)/shard_map/pallas_call | solution.py:627
  159.4 0.6 copy.27
  (3 shorter events, 0.0 us)
Async XLA Ops:
  0.0 3.8 %copy-start = (bf16[256,3584]{1,0:T(8,128)(2,1)S(1)}, bf16[256,3584]{1,0:T(8,128)(2,1)}, u32[]{:S(2)}) copy-start(bf16[256,3584]{1,0:T(8,128)(2,1)} %param.16) | copy-start | bytes 5505028
  0.0 3.4 %copy-start.6 = (bf16[1,128,16,256]{3,2,1,0:T(8,128)(2,1)S(1)}, bf16[1,128,16,256]{3,2,1,0:T(8,128)(2,1)}, u32[]{:S(2)}) copy-start(bf16[1,128,16,256]{3,2,1,0:T(8,128)(2,1)} %param.14) | copy-start | bytes 3145732
  3.7 0.9 copy-start.3
  3.7 0.9 copy-start.4
  3.7 1.0 copy-start.5
  3.8 1.3 copy-start.1
  3.8 1.3 copy-start.2

commit v3 on v2

--- a/solution.py
+++ b/solution.py
@@ -55,10 +55,14 @@
     return mates + [device(1 - role, zh, y, z, x)]
 
 
-def send(src, dst, send_sem, recv_sem, to):
-    copy = pltpu.make_async_remote_copy(
+def remote(src, dst, send_sem, recv_sem, to):
+    return pltpu.make_async_remote_copy(
         src_ref=src, dst_ref=dst, send_sem=send_sem, recv_sem=recv_sem, device_id=to, device_id_type=MESH
     )
+
+
+def send(src, dst, send_sem, recv_sem, to):
+    copy = remote(src, dst, send_sem, recv_sem, to)
     copy.start()
     return copy
 
@@ -70,7 +74,7 @@
         self.s1, self.r1, self.s2, self.r2, self.zs, self.zr = s1, r1, s2, r2, zs, zr
         role, zh, y, z, x = here
         mates = z_mates(z)
-        self.order = [z, mates[1], mates[3], mates[2]] if own_first else [mates[2], mates[3], mates[1], z]
+        self.order = [z, mates[2], mates[3], mates[1]] if own_first else [mates[2], mates[3], mates[1], z]
         self.own = 0 if own_first else 3
         self.zslot = {i: n for n, i in enumerate(i for i in range(4) if i != self.own)}
         self.right, self.left = (x + 1) % 4, (x + 3) % 4
@@ -112,13 +116,12 @@
 
     def end(self, i):
         role, zh, y, z, x = self.here
-        for d in range(2):
-            for h in range(2):
+        n = self.zslot.get(i)
+        for h in range(2):
+            for d in range(2):
                 self.second[i, d, h].wait_recv()
-        if i == self.own:
-            return
-        n = self.zslot[i]
-        for h in range(2):
+            if i == self.own:
+                continue
             self.zt[n, h] = self.line(i, h).astype(BF16)
             self.zcopies[n, h] = send(
                 self.zt.at[n, h],
@@ -171,38 +174,51 @@
 
 
 class PlaneGather:
-    def __init__(self, here, out, half, zs, zr, xs, xr, fs, fr):
-        self.here, self.out, self.half = here, out, half
+    def __init__(self, here, out, half, zs, zr, xs, xr, fs, fr, ls=None):
+        self.here, self.out, self.half, self.ls = here, out, half, ls
         self.zs, self.zr, self.xs, self.xr, self.fs, self.fr = zs, zr, xs, xr, fs, fr
         role, zh, y, z, x = here
         mates = z_mates(z)
-        self.order = [z, mates[1], mates[3], mates[2]]
+        self.order = [z, mates[1], mates[2], mates[3]]
+        self.inner = ((z + 1) // 2) % 2 == 1
+        self.relays = []
         self.to_right = device(role, zh, y, z, (x + 1) % 4)
         self.to_left = device(role, zh, y, z, (x + 3) % 4)
         self.zcopies, self.near, self.far = {}, {}, {}
 
-    def begin(self):
+    def begin(self, halves=(0, 1)):
         role, zh, y, z, x = self.here
         mine = z * 4 + x
-        self.start(0)
-        for m in (1, 2, 3):
-            for h in range(2):
-                block = self.half(self.out, mine, h)
-                self.zcopies[m, h] = send(
+        for h in halves:
+            self.spread(0, h)
+            block = self.half(self.out, mine, h)
+            for m in (1, 2, 3):
+                copy = remote(
                     block, block, self.zs.at[m - 1, h], self.zr.at[m - 1, h], device(role, zh, y, self.order[m], x)
                 )
+                self.zcopies[m, h] = copy
+                if m == 3 and self.ls is not None:
+                    pl.when(self.inner)(copy.start)
+                else:
+                    copy.start()
+
+    def spread(self, i, h):
+        block = self.half(self.out, self.order[i] * 4 + self.here[4], h)
+        for d, to in ((h, (self.to_right, self.to_left)[h]), (1 - h, (self.to_right, self.to_left)[1 - h])):
+            self.near[i, d, h] = send(block, block, self.xs.at[i, d, h], self.xr.at[i, d, h], to)
 
     def start(self, i):
-        x = self.here[4]
-        slot = self.order[i] * 4 + x
-        if i > 0:
-            for h in range(2):
-                self.zcopies[i, h].wait_recv()
         for h in range(2):
-            for d, to in enumerate((self.to_right, self.to_left)):
-                block = self.half(self.out, slot, h if d == 0 else 1 - h)
-                k = h if d == 0 else 1 - h
-                self.near[i, d, k] = send(block, block, self.xs.at[i, d, k], self.xr.at[i, d, k], to)
+            self.zcopies[i, h].wait_recv()
+            self.spread(i, h)
+
+    def relay(self):
+        role, zh, y, z, x = self.here
+        for h in range(2):
+            block = self.half(self.out, self.order[2] * 4 + x, h)
+            copy = remote(block, block, self.ls.at[h], self.zr.at[2, h], device(role, zh, y, self.order[1], x))
+            pl.when(self.inner)(copy.start)
+            self.relays.append(copy)
 
     def pass_on(self, i):
         x = self.here[4]
@@ -218,9 +234,16 @@
             self.far[i, d].wait_recv()
 
     def finish(self):
-        for copies in (self.zcopies, self.near, self.far):
+        for copies in (self.near, self.far):
             for copy in copies.values():
                 copy.wait_send()
+        for (m, h), copy in self.zcopies.items():
+            if m == 3 and self.ls is not None:
+                pl.when(self.inner)(copy.wait_send)
+            else:
+                copy.wait_send()
+        for copy in self.relays:
+            pl.when(self.inner)(copy.wait_send)
 
     def whole(self, between=lambda: None):
         self.begin()
@@ -372,19 +395,6 @@
             at = pl.ds(h * (width // 4), width // 4)
             target[:, at] = dot(chosen, normed[:, at]).astype(BF16)
 
-    for d in (2, 1, 3):
-        yo = (y + d) % 4
-        for q in range(2):
-            pick_into(same.at[q, yo], owner_of(q, yo))
-            sent.append(
-                send(
-                    same.at[q, yo],
-                    got_same.at[role, y],
-                    ref["near"].at[0, d - 1, q],
-                    ref["near"].at[1, d - 1, role],
-                    device(q, zh, yo, z, x),
-                )
-            )
     pick_into(same.at[1 - role, y], owner_of(1 - role, y))
     core = send(
         same.at[1 - role, y], got_same.at[role, y], ref["core"].at[0], ref["core"].at[1], device(1 - role, zh, y, z, x)
@@ -471,38 +481,56 @@
     own_back = pltpu.make_async_copy(made_same.at[role, y], back_same.at[role, y], ref["core"].at[4])
     own_back.start()
 
-    gather = PlaneGather(here, got_cross, lane_half, *[ref[f"c{i}"] for i in range(6)])
+    for d in (1, 3, 2):
+        yo = (y + d) % 4
+        for q in range(2):
+            pick_into(same.at[q, yo], owner_of(q, yo))
+            sent.append(
+                send(
+                    same.at[q, yo],
+                    got_same.at[role, y],
+                    ref["near"].at[0, d - 1, q],
+                    ref["near"].at[1, d - 1, role],
+                    device(q, zh, yo, z, x),
+                )
+            )
+
+    gather = PlaneGather(here, got_cross, lane_half, *[ref[f"c{i}"] for i in range(6)], ls=ref["relay"])
     sums = PlaneSum(here, made_cross, lane_half, *[ref[f"d{i}"] for i in range(11)], own_first=True)
 
     def cross_step(i):
         gather.complete(i)
         cross_experts(gather.order[i])
-        sums.begin(i)
-
-    for one in swaps:
-        one.wait_recv()
-    gather.begin()
+
+    for h in range(2):
+        swaps[h].wait_recv()
+        gather.begin((h,))
     gather.pass_on(0)
     gather.start(1)
     gather.pass_on(1)
-    column_step(1)
     gather.start(2)
+    gather.relay()
     cross_step(0)
+    sums.begin(0)
     gather.pass_on(2)
     gather.start(3)
-    column_step(3)
-    gather.pass_on(3)
     cross_step(1)
     sums.middle(0)
-    column_step(2)
-    sums.end(0)
+    gather.pass_on(3)
+    column_step(1)
     cross_step(2)
+    sums.begin(1)
+    column_step(3)
+    cross_step(3)
+    sums.begin(2)
     sums.middle(1)
+    sums.begin(3)
     sums.end(1)
-    cross_step(3)
     sums.middle(2)
     sums.end(2)
     sums.middle(3)
+    column_step(2)
+    sums.end(0)
     sums.end(3)
     for h in range(2):
         at = pl.ds(h * (half // 2), half // 2)
@@ -519,19 +547,36 @@
     swaps[2].wait_recv()
     swaps[3].wait_recv()
     branches = ref["branches"]
-    per_half = half // tile
-    for i in range(width // tile):
-        at = pl.ds(i * tile, tile)
-        table = back_same[:, :, :, at].reshape(8 * UNIT, tile)
-        value = dot(ref["shared_act"][...], ref["shared_out"][:, at])
-        value = value + dot(ref["gate_high"][...], table) + dot(ref["gate_low"][...], table)
-        table = ref["back_cross"][:, pl.ds((i % per_half) * tile, tile)]
-        routed = dot(ref["cross_high"][...], table) + dot(ref["cross_low"][...], table)
-        value = value + jnp.where(cross_half == i // per_half, routed, 0.0)
-        branches[at, :] = value.T.astype(BF16)
-
     last = PlaneSum(here, branches, flat_half, *[ref[f"e{i}"] for i in range(11)])
-    last.whole()
+    quarter = width // 4
+
+    def combine(i):
+        zz = last.order[i]
+        start = 0
+        for size in (256, 256, 384):
+            at = pl.ds(pl.multiple_of(zz * quarter + start, 128), size)
+            table = back_same[:, :, :, at].reshape(8 * UNIT, size)
+            value = dot(ref["shared_act"][...], ref["shared_out"][:, at])
+            value = value + dot(ref["gate_high"][...], table) + dot(ref["gate_low"][...], table)
+            table = ref["back_cross"][:, pl.ds(pl.multiple_of((zz % 2) * quarter + start, 128), size)]
+            routed = dot(ref["cross_high"][...], table) + dot(ref["cross_low"][...], table)
+            value = value + jnp.where(cross_half == zz // 2, routed, 0.0)
+            branches[at, :] = value.T.astype(BF16)
+            start += size
+        last.begin(i)
+
+    combine(0)
+    combine(1)
+    last.middle(0)
+    combine(2)
+    last.middle(1)
+    combine(3)
+    last.end(0)
+    last.middle(2)
+    last.end(1)
+    last.middle(3)
+    last.end(2)
+    last.end(3)
     for h in range(2):
         value = last.total(h) + flat_half(hidden, mine, h)[...].astype(F32)
         out[pl.ds(h * step, step), :] = value.astype(BF16)
@@ -573,6 +618,7 @@
         "shared_act": vmem((rows, units), BF16),
         "branches": vmem((width, rows), BF16),
         "swap": dma((4, 2)),
+        "relay": dma((2,)),
         "near": dma((2, 3, 2)),
         "back": dma((2, 3, 2)),
         "core": dma((5,)),

time: 162 us -> 144 us (0.89)
  Pallas kernels: 154 us -> 138 us
    pallas_call x1, Pallas kernels: 154 us -> 138 us  [body(): pl.pallas_call(functools.partial(layer_kernel, names), out_shape=jax.Shap...]
where the time goes in v3:
time: 144 us
  Pallas kernels  138 us (96%)
  matrix products  2.8 us (2%)
  local copies, waits for them, and re-layouts  2 us (1%)
    pallas_call x1, Pallas kernels, body(): pl.pallas_call(functools.partial(layer_kernel, names), out_shape=jax.Shap...  138 us

profile of v3, /device:TPU:1, one launch (start us, length us, event | category | flops | bytes accessed | tf_op | source)
XLA Modules:
  0.0 143.6 jit_solution(698112330582653437)
XLA Ops:
  0.0 0.0 copy-start
  0.0 0.0 copy-start.6
  0.0 1.0 reshape.52
  1.0 0.7 iota_compare_fusion
  1.8 1.6 %fusion.11 = (f32[128,2]{1,0:T(8,128)S(1)}, f32[128,2,16]{2,1,0:T(2,128)S(1)}) fusion(pred[128,16]{1,0:T(8,128)(4,1)S(1)} %iota_compare_fusion, bf16[128,2,128]{2,1,0:T(2,128)(2,1)S(1)} %reshape.52, bf16[128,16,256]{2,1,0:T(8,128)(2,1)} %bitcast.32), kind=kOutput, calls=%fused_computation.18 | convolution fusion | flops 1069071 | bytes 640000 | tf_op jit(solution)/shard_map/sub | solution.py:665
  3.4 0.0 copy-done.6
  3.4 0.3 convolution_convert_fusion.1
  3.7 0.0 copy-start.3
  3.7 0.0 copy-start.4
  3.7 0.0 copy-start.5
  3.8 0.0 copy-start.1
  3.8 0.0 copy-start.2
  3.8 0.0 copy-done
  3.8 0.9 fusion.1.part
  4.7 0.0 copy-done.3
  4.7 0.0 copy-done.4
  4.7 0.0 copy-done.5
  4.7 0.3 copy-done.1
  5.0 0.0 copy-done.2
  5.0 137.9 %shard_map.118 = bf16[224,128]{1,0:T(8,128)(2,1)S(1)} custom-call(bf16[3584,128]{1,0:T(8,128)(2,1)S(1)} %fusion.1.part, bf16[224,128]{1,0:T(8,128)(2,1)S(1)} %bitcast.27, f32[1,3584]{1,0:T(1,128)S(1)} %reshape.62.gain, s32[3,128]{1,0:T(4,128)S(1)} %bitcast.29, f32[3,128]{1,0:T(4,128)S(1)} %bitcast.28, bf16[2,2,160,3584]{3,2,1,0:T(8,128)(2,1)} %w_in.1, ...), custom_call_target="tpu_custom_call" | custom-call | tf_op jit(solution)/shard_map/pallas_call | solution.py:673
  143.0 0.6 copy.27
  (3 shorter events, 0.0 us)
Async XLA Ops:
  0.0 3.8 %copy-start = (bf16[256,3584]{1,0:T(8,128)(2,1)S(1)}, bf16[256,3584]{1,0:T(8,128)(2,1)}, u32[]{:S(2)}) copy-start(bf16[256,3584]{1,0:T(8,128)(2,1)} %param.16) | copy-start | bytes 5505028
  0.0 3.4 %copy-start.6 = (bf16[1,128,16,256]{3,2,1,0:T(8,128)(2,1)S(1)}, bf16[1,128,16,256]{3,2,1,0:T(8,128)(2,1)}, u32[]{:S(2)}) copy-start(bf16[1,128,16,256]{3,2,1,0:T(8,128)(2,1)} %param.14) | copy-start | bytes 3145732
  3.7 0.9 copy-start.3
  3.7 0.9 copy-start.4
  3.7 1.0 copy-start.5
  3.8 1.3 copy-start.1
  3.8 1.3 copy-start.2

commit v4 on v3

--- a/solution.py
+++ b/solution.py
@@ -16,7 +16,7 @@
 MESH = pl.DeviceIdType.MESH
 BF16 = jnp.bfloat16
 F32 = jnp.float32
-VMEM_LIMIT = 50 * 1024 * 1024
+VMEM_LIMIT = 63 * 1024 * 1024
 
 
 def places():
@@ -289,14 +289,14 @@
 
 
 def slot_rows(routes):
-    count = routes.shape[1]
+    count = routes[0].shape[1]
     ids = lax.broadcasted_iota(jnp.int32, (EXPERTS, count), 0)
-    named = [ids == routes[k : k + 1, :] for k in range(TOPK)]
+    named = [ids == one for one in routes]
     chosen = jnp.where(named[0] | named[1] | named[2], 1.0, 0.0).astype(BF16)
     earlier = lax.broadcasted_iota(jnp.int32, (count, count), 0) < lax.broadcasted_iota(jnp.int32, (count, count), 1)
     before = dot(chosen, jnp.where(earlier, 1.0, 0.0).astype(BF16))
     place = [jnp.sum(jnp.where(one, before, 0.0), axis=0, keepdims=True).astype(jnp.int32) for one in named]
-    return [routes[k : k + 1, :] * CAP + place[k] for k in range(TOPK)]
+    return [routes[k] * CAP + place[k] for k in range(TOPK)]
 
 
 def unit_hits(slots, owner):
@@ -304,23 +304,61 @@
     return [ids == one for one in slots]
 
 
-def layer_kernel(names, part, resid, gain, routes, gates, w_in, w_out, s_in, s_out, out, *scratch):
+def same_place(count):
+    place = [lax.broadcasted_iota(jnp.int32, (count, count), d) for d in range(2)]
+    return jnp.where(place[0] == place[1], 1.0, 0.0).astype(BF16)
+
+
+def attend(queries, kv, lengths, context):
+    rows = queries.shape[0]
+    block = 32
+    place = [lax.broadcasted_iota(jnp.int32, (rows, rows), d) for d in range(2)]
+    live = jnp.where(place[0] == place[1], lengths[...].astype(F32), 0.0)
+    live = jnp.sum(live, axis=1, keepdims=True).astype(jnp.int32)
+    ahead = lax.broadcasted_iota(jnp.int32, (block, block * L), 1) - L * lax.broadcasted_iota(
+        jnp.int32, (block, block * L), 0
+    )
+    parts = [(start, head) for start in range(0, rows, block) for head in range(queries.shape[1] // HD)]
+    scores = [
+        dot_rows(queries[start : start + block, head * HD : (head + 1) * HD], kv[start * L : (start + block) * L, :HD])
+        * HD ** (-0.5)
+        for start, head in parts
+    ]
+    weights = []
+    for (start, _), score in zip(parts, scores):
+        visible = (ahead >= 0) & (ahead < live[start : start + block])
+        score = jnp.where(visible, score, -1e30)
+        maximum = jnp.max(score, axis=1, keepdims=True)
+        exponent = jnp.where(visible, jnp.exp(score - maximum), 0.0)
+        weights.append((exponent / jnp.sum(exponent, axis=1, keepdims=True)).astype(BF16))
+    for (start, head), weight in zip(parts, weights):
+        values = kv[start * L : (start + block) * L, HD:]
+        context[start : start + block, head * HD : (head + 1) * HD] = dot(weight, values).astype(BF16)
+
+
+def layer_kernel(
+    names, gain, len_in, routes_in, gates_in, q_in, kv_in, resid_in, o_proj, w_in, w_out, s_in, s_out, out, *scratch
+):
     ref = dict(zip(names, scratch))
     here = places()
     role, zh, y, z, x = here
     mine = z * 4 + x
-    rows = routes.shape[1]
-    width = gain.shape[1]
+    rows = routes_in.shape[2]
+    width = gain.shape[0]
     half = width // 2
     units = w_in.shape[2]
     to, source = partners(*here)
 
-    barrier = pltpu.get_barrier_semaphore()
-    mates = plane_mates(*here) + column_mates(*here) + [to, source]
-    for one in mates:
-        pl.semaphore_signal(barrier, inc=1, device_id=one, device_id_type=MESH)
-
-    loads = []
+    queries, kv, resid = ref["queries"], ref["kv"], ref["resid"]
+    loads = [
+        (len_in, ref["lengths"]),
+        (q_in, queries),
+        (kv_in, kv),
+        (o_proj, ref["out_proj"]),
+        (routes_in, ref["routes"]),
+        (gates_in, ref["gates"]),
+        (resid_in, resid),
+    ]
     for j in range(2):
         loads.append((w_in.at[j, 0], ref["gate"].at[pl.ds(j * units, units), :]))
         loads.append((w_in.at[j, 1], ref["up"].at[pl.ds(j * units, units), :]))
@@ -328,11 +366,51 @@
         loads.append((s_in.at[j], ref["shared_in"].at[j]))
     loads.append((s_out, ref["shared_out"]))
     loads = [pltpu.make_async_copy(a, b, ref["load"].at[i]) for i, (a, b) in enumerate(loads)]
-    for one in loads:
+    for one in loads[:4]:
         one.start()
-
-    slots = slot_rows(routes[...])
-    gate_rows = gates[...]
+    barrier = pltpu.get_barrier_semaphore()
+    mates = plane_mates(*here) + column_mates(*here) + [to, source]
+    for one in mates:
+        pl.semaphore_signal(barrier, inc=1, device_id=one, device_id_type=MESH)
+
+    for one in loads[4:]:
+        one.start()
+
+
+    cross_owner = flip(role, x % 2) * 8 + (1 - zh) * 4 + xor4(y, z)
+    cross_half = x // 2
+
+    for one in loads[:3]:
+        one.wait()
+    attend(queries, kv, ref["lengths"], ref["context"])
+
+    eye = same_place(rows)
+    quarter = width // 4
+    first = PlaneSum(here, ref["attended"], flat_half, *[ref[f"a{i}"] for i in range(11)])
+    loads[3].wait()
+
+    def project(i):
+        start = 0
+        for size in (256, 256, 384):
+            at = pl.ds(pl.multiple_of(first.order[i] * quarter + start, 128), size)
+            ref["attended"][at, :] = dot(ref["context"][...], ref["out_proj"][:, at]).T.astype(BF16)
+            start += size
+
+    project(0)
+    pl.semaphore_wait(barrier, len(mates))
+    first.begin(0)
+    project(1)
+    first.begin(1)
+    project(2)
+    first.begin(2)
+    first.middle(0)
+    project(3)
+    first.begin(3)
+
+    for one in loads[4:7]:
+        one.wait()
+    slots = slot_rows([ref["routes"][k] for k in range(TOPK)])
+    gate_rows = [ref["gates"][k] for k in range(TOPK)]
 
     def pick(owner):
         hits = unit_hits(slots, owner)
@@ -340,17 +418,25 @@
 
     def weigh(owner):
         hits = unit_hits(slots, owner)
-        return sum(jnp.where(hits[k], gate_rows[k : k + 1, :], 0.0) for k in range(TOPK))
+        return sum(jnp.where(hits[k], gate_rows[k], 0.0) for k in range(TOPK))
 
     def owner_of(q, yo):
         return q * 8 + zh * 4 + yo
 
-    cross_owner = flip(role, x % 2) * 8 + (1 - zh) * 4 + xor4(y, z)
-    cross_half = x // 2
-
-    pl.semaphore_wait(barrier, len(mates))
-    first = PlaneSum(here, part, flat_half, *[ref[f"a{i}"] for i in range(11)])
-    first.whole()
+    for q in range(2):
+        for yo in range(4):
+            at = pl.ds((q * 4 + yo) * UNIT, UNIT)
+            ref["weights"][at, :] = weigh(owner_of(q, yo))
+    ref["gate_high"][...], ref["gate_low"][...] = split(ref["weights"][...].T)
+    ref["cross_high"][...], ref["cross_low"][...] = split(weigh(cross_owner).T)
+
+    first.middle(1)
+    first.end(0)
+    first.middle(2)
+    first.end(1)
+    first.middle(3)
+    first.end(2)
+    first.end(3)
     hidden = ref["hidden"]
     step = resid.shape[0] // 2
     for h in range(2):
@@ -362,13 +448,13 @@
     tile = 256
     square = jnp.zeros((rows, 1), F32)
     for i in range(width // tile):
-        wide = hidden[pl.ds(i * tile, tile), :].astype(F32).T
+        wide = dot_rows(eye, hidden[pl.ds(i * tile, tile), :])
         square = square + jnp.sum(wide * wide, axis=1, keepdims=True)
         normed[:, pl.ds(i * tile, tile)] = wide.astype(BF16)
     scale = lax.rsqrt(square / width + 1e-06)
     for i in range(width // tile):
         at = pl.ds(i * tile, tile)
-        normed[:, at] = (normed[:, at].astype(F32) * scale * gain[:, at]).astype(BF16)
+        normed[:, at] = (normed[:, at].astype(F32) * scale * gain[at].astype(F32).reshape(1, tile)).astype(BF16)
 
     chosen = pick(cross_owner)
     got_cross = ref["got_cross"]
@@ -401,15 +487,9 @@
     )
     pick_into(got_same.at[role, y], owner_of(role, y))
 
-    for one in loads:
+    for one in loads[7:]:
         one.wait()
 
-    for q in range(2):
-        for yo in range(4):
-            at = pl.ds((q * 4 + yo) * UNIT, UNIT)
-            ref["weights"][at, :] = weigh(owner_of(q, yo))
-    ref["gate_high"][...], ref["gate_low"][...] = split(ref["weights"][...].T)
-    ref["cross_high"][...], ref["cross_low"][...] = split(weigh(cross_owner).T)
     pre = [dot_rows(normed[...], ref["shared_in"][g]) for g in range(2)]
     ref["shared_act"][...] = (jax.nn.silu(pre[0]) * pre[1]).astype(BF16)
 
@@ -525,11 +605,11 @@
     sums.begin(2)
     sums.middle(1)
     sums.begin(3)
+    column_step(2)
     sums.end(1)
     sums.middle(2)
     sums.end(2)
     sums.middle(3)
-    column_step(2)
     sums.end(0)
     sums.end(3)
     for h in range(2):
@@ -548,7 +628,6 @@
     swaps[3].wait_recv()
     branches = ref["branches"]
     last = PlaneSum(here, branches, flat_half, *[ref[f"e{i}"] for i in range(11)])
-    quarter = width // 4
 
     def combine(i):
         zz = last.order[i]
@@ -588,7 +667,7 @@
         one.wait_send()
 
 
-def layer_scratch(rows, width, units, tp_count):
+def layer_scratch(rows, width, heads_width, units, tp_count):
     half, part = width // 2, width // tp_count
     small, large = (part // 2, rows), (UNIT, half // 2)
     dma, vmem = pltpu.SemaphoreType.DMA, pltpu.VMEM
@@ -598,7 +677,16 @@
         "down": vmem((2 * units, width), BF16),
         "shared_in": vmem((2, units, width), BF16),
         "shared_out": vmem((units, width), BF16),
-        "load": dma((9,)),
+        "load": dma((16,)),
+        "routes": vmem((TOPK, 1, rows), jnp.int32),
+        "gates": vmem((TOPK, 1, rows), F32),
+        "lengths": vmem((1, rows), jnp.int32),
+        "queries": vmem((rows, heads_width), BF16),
+        "kv": vmem((rows * L, 2 * HD), BF16),
+        "resid": vmem((part, rows), BF16),
+        "out_proj": vmem((heads_width, width), BF16),
+        "context": vmem((rows, heads_width), BF16),
+        "attended": vmem((width, rows), BF16),
         "hidden": vmem((width, rows), BF16),
         "normed": vmem((rows, width), BF16),
         "cross": vmem((UNIT, half), BF16),
@@ -652,37 +740,26 @@
     part = residual.shape[2]
     tp_count = lax.axis_size("tp")
     width = part * tp_count
-    head_count = queries.shape[2] // HD
-
-    query_heads = queries.reshape(rows, head_count, HD)
-    cache_rows = kv_cache.reshape(rows, L, 2 * HD)
-    cache_keys = cache_rows[:, :, :HD]
-    cache_values = cache_rows[:, :, HD:]
-    scores = jnp.einsum("rhd,rld->rhl", query_heads, cache_keys, preferred_element_type=F32) * HD ** (-0.5)
-    visible = jnp.arange(L, dtype=jnp.int32)[None, None, :] < cache_lengths.reshape(rows)[:, None, None]
-    scores = jnp.where(visible, scores, -1e30)
-    maximum = jnp.max(scores, axis=-1, keepdims=True)
-    exponent = jnp.where(visible, jnp.exp(scores - maximum), 0.0)
-    attn_weights = (exponent / jnp.sum(exponent, axis=-1, keepdims=True)).astype(BF16)
-    context = jnp.einsum("rhl,rld->rhd", attn_weights, cache_values, preferred_element_type=F32).astype(BF16)
-    context = context.reshape(rows, head_count * HD)
-    attended = jnp.einsum("kd,rk->dr", out_proj, context, preferred_element_type=F32).astype(BF16)
-
-    names, scratch = layer_scratch(rows, width, expert_out.shape[1], tp_count)
-    vmem, hbm = pl.BlockSpec(memory_space=pltpu.VMEM), pl.BlockSpec(memory_space=pl.ANY)
+    heads_width = queries.shape[2]
+
+    names, scratch = layer_scratch(rows, width, heads_width, expert_out.shape[1], tp_count)
+    vmem, hbm = pl.BlockSpec(memory_space=pltpu.VMEM), pl.BlockSpec(memory_space=pltpu.HBM)
     layer_out = pl.pallas_call(
         functools.partial(layer_kernel, names),
         out_shape=jax.ShapeDtypeStruct((part, rows), BF16),
-        in_specs=[vmem] * 5 + [hbm] * 4,
+        in_specs=[vmem] + [hbm] * 11,
         out_specs=vmem,
         scratch_shapes=scratch,
         compiler_params=pltpu.CompilerParams(collective_id=1, has_side_effects=True, vmem_limit_bytes=VMEM_LIMIT),
     )(
-        attended,
+        norm_gain,
+        cache_lengths.reshape(1, rows),
+        jnp.transpose(routes.reshape(1, rows, TOPK), (2, 0, 1)),
+        jnp.transpose(gate_weights.reshape(1, rows, TOPK), (2, 0, 1)),
+        queries.reshape(rows, heads_width),
+        kv_cache.reshape(rows * L, 2 * HD),
         residual.reshape(rows, part).T,
-        norm_gain.astype(F32).reshape(1, width),
-        routes.reshape(rows, TOPK).T,
-        gate_weights.reshape(rows, TOPK).T,
+        out_proj,
         expert_in,
         expert_out,
         shared_in,

time: 144 us -> 138 us (0.958)
  matrix products: 2.8 us -> 0 us
  Pallas kernels: 138 us -> 136 us
    pallas_call x1, Pallas kernels: 138 us -> 136 us  [body(): pl.pallas_call(functools.partial(layer_kernel, names), out_shape=jax.Shap...]
    sub x1 -> x0, matrix products: 1.6 us -> none  [body(): exponent = jnp.where(visible, jnp.exp(scores - maximum), 0.0)]
where the time goes in v4:
time: 138 us; the launch traced here: 137 us
  Pallas kernels  136 us (99%)
  local copies, waits for them, and re-layouts  1.45 us (1%)
    pallas_call x1, Pallas kernels, body(): pl.pallas_call(functools.partial(layer_kernel, names), out_shape=jax.Shap...  136 us

profile of v4, /device:TPU:1, one launch (start us, length us, event | category | flops | bytes accessed | tf_op | source)
XLA Modules:
  0.0 137.5 jit_solution(7447393256850877711)
XLA Ops:
  0.0 136.0 %shard_map.118 = bf16[224,128]{1,0:T(8,128)(2,1)} custom-call(bf16[3584]{0:T(1024)(128)(2,1)} %gain.1, s32[1,128]{1,0:T(1,128)} %len_in.1, s32[3,1,128]{2,1,0:T(1,128)} %bitcast.14, f32[3,1,128]{2,1,0:T(1,128)} %bitcast.15, bf16[128,256]{1,0:T(8,128)(2,1)} %bitcast.12, bf16[2048,256]{1,0:T(8,128)(2,1)} %bitcast.10, bf16[224,128]{1,0:T(8,128)(2,1)} %bitcast.13, ...), custom_call_target="tpu_custom_call" | custom-call | tf_op jit(solution)/shard_map/pallas_call | solution.py:747
  136.0 1.4 %copy.14 = bf16[1,128,224]{1,2,0:T(8,128)(2,1)} copy(bf16[1,128,224]{1,2,0:T(8,128)(2,1)} %bitcast.11) | data formatting | bytes 114688

commit v5 on v4

--- a/solution.py
+++ b/solution.py
@@ -347,6 +347,7 @@
     width = gain.shape[0]
     half = width // 2
     units = w_in.shape[2]
+    up_at = up_place(units)
     to, source = partners(*here)
 
     queries, kv, resid = ref["queries"], ref["kv"], ref["resid"]
@@ -360,8 +361,8 @@
         (resid_in, resid),
     ]
     for j in range(2):
-        loads.append((w_in.at[j, 0], ref["gate"].at[pl.ds(j * units, units), :]))
-        loads.append((w_in.at[j, 1], ref["up"].at[pl.ds(j * units, units), :]))
+        loads.append((w_in.at[j, 0], ref["gate_up"].at[pl.ds(j * units, units), :]))
+        loads.append((w_in.at[j, 1], ref["gate_up"].at[pl.ds(up_at + j * units, units), :]))
         loads.append((w_out.at[j], ref["down"].at[pl.ds(j * units, units), :]))
         loads.append((s_in.at[j], ref["shared_in"].at[j]))
     loads.append((s_out, ref["shared_out"]))
@@ -375,6 +376,9 @@
 
     for one in loads[4:]:
         one.start()
+    unused = up_at - 2 * units
+    if unused:
+        ref["gate_up"][pl.ds(2 * units, unused), :] = jnp.zeros((unused, width), BF16)
 
 
     cross_owner = flip(role, x % 2) * 8 + (1 - zh) * 4 + xor4(y, z)
@@ -446,15 +450,15 @@
 
     normed = ref["normed"]
     tile = 256
-    square = jnp.zeros((rows, 1), F32)
+    square = jnp.zeros((1, rows), F32)
     for i in range(width // tile):
-        wide = dot_rows(eye, hidden[pl.ds(i * tile, tile), :])
-        square = square + jnp.sum(wide * wide, axis=1, keepdims=True)
-        normed[:, pl.ds(i * tile, tile)] = wide.astype(BF16)
-    scale = lax.rsqrt(square / width + 1e-06)
+        wide = hidden[pl.ds(i * tile, tile), :].astype(F32)
+        square = square + jnp.sum(wide * wide, axis=0, keepdims=True)
+    scale = jnp.sum(jnp.where(eye > 0, lax.rsqrt(square / width + 1e-06), 0.0), axis=1, keepdims=True)
     for i in range(width // tile):
         at = pl.ds(i * tile, tile)
-        normed[:, at] = (normed[:, at].astype(F32) * scale * gain[at].astype(F32).reshape(1, tile)).astype(BF16)
+        wide = dot_rows(eye, hidden[at, :])
+        normed[:, at] = (wide * scale * gain[at].astype(F32).reshape(1, tile)).astype(BF16)
 
     chosen = pick(cross_owner)
     got_cross = ref["got_cross"]
@@ -501,8 +505,8 @@
     def experts(load, store):
         at = [pl.ds(h * half, half) for h in range(2)]
         found = [load(h) for h in range(2)]
-        gate_pre = sum(dot_rows(found[h], ref["gate"][:, at[h]]) for h in range(2))
-        up_pre = sum(dot_rows(found[h], ref["up"][:, at[h]]) for h in range(2))
+        pre = sum(dot_rows(found[h], ref["gate_up"][:, at[h]]) for h in range(2))
+        gate_pre, up_pre = pre[:, : 2 * units], pre[:, up_at:]
         act = jnp.where(own_expert, jax.nn.silu(gate_pre) * up_pre, 0.0).astype(BF16)
         for h in range(2):
             for c in range(2):
@@ -549,18 +553,6 @@
                 )
             )
 
-    core.wait_recv()
-    same_experts(y)
-    core_back = send(
-        made_same.at[1 - role, y],
-        back_same.at[role, y],
-        ref["core"].at[2],
-        ref["core"].at[3],
-        device(1 - role, zh, y, z, x),
-    )
-    own_back = pltpu.make_async_copy(made_same.at[role, y], back_same.at[role, y], ref["core"].at[4])
-    own_back.start()
-
     for d in (1, 3, 2):
         yo = (y + d) % 4
         for q in range(2):
@@ -574,6 +566,18 @@
                     device(q, zh, yo, z, x),
                 )
             )
+
+    core.wait_recv()
+    same_experts(y)
+    core_back = send(
+        made_same.at[1 - role, y],
+        back_same.at[role, y],
+        ref["core"].at[2],
+        ref["core"].at[3],
+        device(1 - role, zh, y, z, x),
+    )
+    own_back = pltpu.make_async_copy(made_same.at[role, y], back_same.at[role, y], ref["core"].at[4])
+    own_back.start()
 
     gather = PlaneGather(here, got_cross, lane_half, *[ref[f"c{i}"] for i in range(6)], ls=ref["relay"])
     sums = PlaneSum(here, made_cross, lane_half, *[ref[f"d{i}"] for i in range(11)], own_first=True)
@@ -597,6 +601,7 @@
     cross_step(1)
     sums.middle(0)
     gather.pass_on(3)
+    sums.begin(3)
     column_step(1)
     cross_step(2)
     sums.begin(1)
@@ -604,7 +609,6 @@
     cross_step(3)
     sums.begin(2)
     sums.middle(1)
-    sums.begin(3)
     column_step(2)
     sums.end(1)
     sums.middle(2)
@@ -667,13 +671,16 @@
         one.wait_send()
 
 
+def up_place(units):
+    return -(-2 * units // 128) * 128
+
+
 def layer_scratch(rows, width, heads_width, units, tp_count):
     half, part = width // 2, width // tp_count
     small, large = (part // 2, rows), (UNIT, half // 2)
     dma, vmem = pltpu.SemaphoreType.DMA, pltpu.VMEM
     named = {
-        "gate": vmem((2 * units, width), BF16),
-        "up": vmem((2 * units, width), BF16),
+        "gate_up": vmem((up_place(units) + 2 * units, width), BF16),
         "down": vmem((2 * units, width), BF16),
         "shared_in": vmem((2, units, width), BF16),
         "shared_out": vmem((units, width), BF16),

time: 138 us -> 135 us (0.978)
  Pallas kernels: 136 us -> 133 us
    pallas_call x1, Pallas kernels: 136 us -> 133 us  [body(): pl.pallas_call(functools.partial(layer_kernel, names), out_shape=jax.Shap...]
where the time goes in v5:
time: 135 us
  Pallas kernels  133 us (99%)
  local copies, waits for them, and re-layouts  1.45 us (1%)
    pallas_call x1, Pallas kernels, body(): pl.pallas_call(functools.partial(layer_kernel, names), out_shape=jax.Shap...  133 us

profile of v5, /device:TPU:1, one launch (start us, length us, event | category | flops | bytes accessed | tf_op | source)
XLA Modules:
  0.0 134.6 jit_solution(284455995075043089)
XLA Ops:
  0.0 133.1 %shard_map.118 = bf16[224,128]{1,0:T(8,128)(2,1)} custom-call(bf16[3584]{0:T(1024)(128)(2,1)} %gain.1, s32[1,128]{1,0:T(1,128)} %len_in.1, s32[3,1,128]{2,1,0:T(1,128)} %bitcast.14, f32[3,1,128]{2,1,0:T(1,128)} %bitcast.15, bf16[128,256]{1,0:T(8,128)(2,1)} %bitcast.12, bf16[2048,256]{1,0:T(8,128)(2,1)} %bitcast.10, bf16[224,128]{1,0:T(8,128)(2,1)} %bitcast.13, ...), custom_call_target="tpu_custom_call" | custom-call | tf_op jit(solution)/shard_map/pallas_call | solution.py:754
  133.1 1.4 %copy.14 = bf16[1,128,224]{1,2,0:T(8,128)(2,1)} copy(bf16[1,128,224]{1,2,0:T(8,128)(2,1)} %bitcast.11) | data formatting | bytes 114688
